TPU v7x, 128 devices: a whole 4x4x4 slice. The times are simulated.
128 devices in a mesh: rec: 8 (over y, core), tm: 16 (over x, z).
Axes of the slice: x: 4, y: 4, z: 4, core: 2. Of those that a mesh axis runs over, the one named last changes fastest.
Arguments:
- loader_rows: bfloat16 [8, 32768, 1024], P('rec', 'tm'), may hold values from -6 to 6
- frame_counts: int32 [8, 16, 16], P('rec'), may hold values from 0 to 128, as said below
- lengths: int32 [8], P('rec'), may hold values from 8193 to 16384, as said below
- cotangent: bfloat16 [8, 16384, 1024], P('rec', 'tm'), may hold values from -6 to 6
- norm_gain: float32 [1024], replicated, may hold values from 0.5 to 1.5
- w_expand: bfloat16 [1024, 2048], replicated, may hold values from -0.1875 to 0.1875
- conv_taps: float32 [9, 1024], replicated, may hold values from -2 to 2
- conv_gain: float32 [1024], replicated, may hold values from 0.5 to 1.5
- w_project: bfloat16 [1024, 1024], replicated, may hold values from -0.1875 to 0.1875
Outputs:
- layer_out: bfloat16 [8, 16384, 1024], P('rec', 'tm')
- grad_in: bfloat16 [8, 16384, 1024], P('rec', 'tm')
- grad_expand: float32 [1024, 2048], P('tm')
- grad_project: float32 [1024, 1024], P('tm')
- grad_taps: float32 [9, 1024], replicated
- grad_norm_gain: float32 [1024], replicated
- grad_conv_gain: float32 [1024], replicated
Inputs may be any that keep to these rules, and one draw needn't show every extreme that they name: frame_counts[r, j, k] rows of bucket (j, k) are live, in its first slots; the other slots hold values that are not part of the recording. For every r and k the counts sum over j to exactly 1024, and in every such column some source fills its bucket with 128 rows. `lengths`: in every draw some recording has all 16384 frames.
All inputs are finite; a program needn't handle non-finite values.
Results may differ from a plain program's by a relative error of at most 0.0062.
Values may be sent and summed in bfloat16 or wider, within the bound.
A program may use at most 128 MiB of HBM per device.

v0:
```python
import jax
import jax.numpy as jnp
from jax import lax
from jax.sharding import PartitionSpec as P

EPS = 1e-05


def with_halo(value, sides, width):
    for axis, dim in sides:
        size, length = (lax.axis_size(axis), value.shape[dim])
        up = [(i, (i + 1) % size) for i in range(size - 1)]
        down = [(j, i) for i, j in up]
        last = lax.slice_in_dim(value, length - width, length, axis=dim)
        first = lax.slice_in_dim(value, 0, width, axis=dim)
        before = lax.ppermute(last, axis, up)
        after = lax.ppermute(first, axis, down)
        value = jnp.concatenate([before, value, after], axis=dim)
    return value


def normalize(values):
    center = values - jnp.mean(values, axis=-1, keepdims=True)
    inverse = lax.rsqrt(jnp.mean(center * center, axis=-1, keepdims=True) + EPS)
    return (center * inverse, inverse)


def norm_back(grad_norm, normed, inverse):
    return inverse * (
        grad_norm
        - jnp.mean(grad_norm, axis=-1, keepdims=True)
        - normed * jnp.mean(grad_norm * normed, axis=-1, keepdims=True)
    )


def contract_rows(left, right):
    return lax.dot_general(
        left, right, (((0,), (0,)), ((), ())), preferred_element_type=jnp.float32
    )


def contract_cols(left, right):
    return lax.dot_general(
        left, right, (((1,), (1,)), ((), ())), preferred_element_type=jnp.float32
    )


def per_device(
    loader_rows,
    frame_counts,
    lengths,
    cotangent,
    norm_gain,
    w_expand,
    conv_taps,
    conv_gain,
    w_project,
):
    shards = lax.axis_size("tm")
    shard_index = lax.axis_index("tm")
    channels = norm_gain.shape[0]
    frames = cotangent.shape[1]
    capacity = loader_rows.shape[1] // shards
    taps_count = conv_taps.shape[0]
    margin = taps_count // 2
    buckets = loader_rows[0].reshape(shards, capacity, channels)
    arrived = lax.all_to_all(buckets, "tm", split_axis=0, concat_axis=0, tiled=True).reshape(
        shards * capacity, channels
    )
    shard_ids = jnp.arange(shards, dtype=jnp.int32)
    column = jnp.sum(jnp.where(shard_ids[None, :] == shard_index, frame_counts[0], 0), axis=1)
    run_ends = jnp.cumsum(column)
    starts = run_ends - column
    position = jnp.arange(frames, dtype=jnp.int32)
    source = jnp.sum((run_ends[:, None] <= position[None, :]).astype(jnp.int32), axis=0)
    picked = source[:, None] == shard_ids[None, :]
    first_slot = jnp.sum(jnp.where(picked, starts[None, :], 0), axis=1)
    row_index = source * capacity + position - first_slot
    sequence = jnp.take(arrived, row_index, axis=0)
    valid_mask = (shard_index * frames + position < lengths[0]).astype(jnp.float32)[:, None]
    inputs = sequence.astype(jnp.float32)
    normed_in, inverse_in = normalize(inputs)
    scaled_in = (normed_in * norm_gain).astype(jnp.bfloat16)
    expanded = jnp.dot(scaled_in, w_expand, preferred_element_type=jnp.float32)
    linear = expanded[:, :channels]
    gate_sig = jax.nn.sigmoid(expanded[:, channels:])
    glu_out = (linear * gate_sig * valid_mask).astype(jnp.bfloat16)
    glu_rim = with_halo(glu_out, (("tm", 0),), margin)
    depthwise = jnp.zeros((frames, channels), jnp.float32)
    for kernel_tap in range(taps_count):
        depthwise = depthwise + conv_taps[kernel_tap] * glu_rim[
            kernel_tap : kernel_tap + frames
        ].astype(jnp.float32)
    normed_conv, inverse_conv = normalize(depthwise)
    scaled_conv = normed_conv * conv_gain
    swish_sig = jax.nn.sigmoid(scaled_conv)
    swished = (scaled_conv * swish_sig).astype(jnp.bfloat16)
    projected = jnp.dot(swished, w_project, preferred_element_type=jnp.float32)
    layer_out = ((inputs + projected) * valid_mask).astype(jnp.bfloat16)
    cot_rec = cotangent[0]
    grad_out = jnp.where(valid_mask > 0.5, cot_rec, jnp.zeros_like(cot_rec))
    grad_project = contract_rows(swished, grad_out)
    grad_swished = contract_cols(grad_out, w_project)
    grad_scaled_conv = grad_swished * swish_sig * (1.0 + scaled_conv * (1.0 - swish_sig))
    grad_conv_gain = jnp.sum(grad_scaled_conv * normed_conv, axis=0)
    grad_depth = norm_back(grad_scaled_conv * conv_gain, normed_conv, inverse_conv)
    depth_rim = with_halo(grad_depth, (("tm", 0),), margin)
    grad_taps = jnp.stack(
        [
            jnp.sum(
                grad_depth * glu_rim[kernel_tap : kernel_tap + frames].astype(jnp.float32), axis=0
            )
            for kernel_tap in range(taps_count)
        ]
    )
    grad_glu = jnp.zeros((frames, channels), jnp.float32)
    for kernel_tap in range(taps_count):
        offset = 2 * margin - kernel_tap
        grad_glu = grad_glu + conv_taps[kernel_tap] * depth_rim[offset : offset + frames]
    grad_glu = grad_glu * valid_mask
    grad_expanded = jnp.concatenate(
        [grad_glu * gate_sig, grad_glu * linear * gate_sig * (1.0 - gate_sig)], axis=1
    ).astype(jnp.bfloat16)
    grad_expand = contract_rows(scaled_in, grad_expanded)
    grad_scaled_in = contract_cols(grad_expanded, w_expand)
    grad_norm_gain = jnp.sum(grad_scaled_in * normed_in, axis=0)
    grad_in = (
        grad_out.astype(jnp.float32) + norm_back(grad_scaled_in * norm_gain, normed_in, inverse_in)
    ).astype(jnp.bfloat16)
    small_sums = lax.psum((grad_taps, grad_norm_gain, grad_conv_gain), ("rec", "tm"))
    share_rows = channels // shards
    total_expand, total_project = lax.psum((grad_expand, grad_project), ("rec", "tm"))
    share_expand = lax.dynamic_slice_in_dim(total_expand, shard_index * share_rows, share_rows, 0)
    share_project = lax.dynamic_slice_in_dim(total_project, shard_index * share_rows, share_rows, 0)
    return (
        layer_out[None],
        grad_in[None],
        share_expand,
        share_project,
        small_sums[0],
        small_sums[1],
        small_sums[2],
    )


def solution(mesh):
    return jax.shard_map(
        per_device,
        mesh=mesh,
        in_specs=(
            P("rec", "tm", None),
            P("rec", None, None),
            P("rec"),
            P("rec", "tm", None),
            P(),
            P(),
            P(),
            P(),
            P(),
        ),
        out_specs=(
            P("rec", "tm", None),
            P("rec", "tm", None),
            P("tm", None),
            P("tm", None),
            P(),
            P(),
            P(),
        ),
        check_vma=False,
    )
```

profile of v0, /device:TPU:1, one launch (start us, length us, event | category | flops | bytes accessed | tf_op | source)
XLA Modules:
  0.0 349.5 jit_solution(10136296833171916788)
XLA Ops:
  7.2 0.0 copy-start
  7.2 0.0 copy-start.9
  7.2 0.0 copy-start.8
  7.2 8.6 %all-to-all-start = ((bf16[16,128,1024]{2,1,0:T(8,128)(2,1)}), bf16[16,128,1024]{2,1,0:T(8,128)(2,1)}, u32[]{:S(2)}, u32[]{:S(2)}) async-start(bf16[16,128,1024]{2,1,0:T(8,128)(2,1)} %bitcast.49), calls=%async_computation | async-start | bytes 8388608 | tf_op jit(solution)/shard_map/all_to_all | solution.py:67
  15.8 0.0 all-reduce.4.cloned.1.call-start
  16.5 0.0 copy-done.9
  16.6 0.1 fusion.69
  16.7 0.1 copy.22
  16.8 0.1 reduce
  16.9 0.1 convert_reduce_fusion.1
  17.0 0.1 select_reduce_fusion
  17.2 0.0 copy-done.8
  17.2 60.1 %all-to-all-done = bf16[16,128,1024]{2,1,0:T(8,128)(2,1)} async-done(((bf16[16,128,1024]{2,1,0:T(8,128)(2,1)}), bf16[16,128,1024]{2,1,0:T(8,128)(2,1)}, u32[]{:S(2)}, u32[]{:S(2)}) %all-to-all-start) | async-done | bytes 4194336 | tf_op jit(solution)/shard_map/all_to_all | solution.py:67
  77.3 8.7 %gather_fusion = bf16[1024,1024]{1,0:T(8,128)(2,1)} fusion(bf16[2048,1024]{1,0:T(8,128)(2,1)} %bitcast.3, s32[1024]{0:T(1024)S(1)} %broadcast_clamp_fusion), kind=kCustom, calls=%fused_computation | custom fusion | bytes 4198400 | tf_op jit(solution)/shard_map/jit(_take)/gather | solution.py:79
  86.1 0.0 copy-start.1
  86.1 2.3 convert_reduce_fusion
  88.4 2.4 fusion.13
  90.9 0.0 copy-done.1
  90.9 0.0 copy-done.11
  90.9 7.2 %fusion.75 = f32[1024,2048]{1,0:T(8,128)S(1)} fusion(bf16[1024,2048]{1,0:T(8,128)(2,1)} %param.14, f32[1024]{0:T(1024)S(1)} %copy-done.11, f32[1024]{0:T(1024)S(1)} %add_rsqrt_fusion.1, f32[1024]{0:T(1024)S(1)} %broadcast_multiply_fusion.5, bf16[1024,1024]{1,0:T(8,128)(2,1)S(1)} %copy-done.1, pred[1024]{0:T(1024)(128)(4,1)S(1)} %compare_and_fusion), kind=kOutput, calls=%fused_computation.154 | convolution fusion | flops 4301258752 | bytes 14693376 | tf_op jit(solution)/shard_map/dot_general | solution.py:84
  98.1 1.6 multiply_convert_fusion.3
  99.7 1.3 collective-permute-start
  101.0 1.5 collective-permute-start.1
  102.5 0.0 collective-permute-done
  102.5 2.9 collective-permute-done.1
  105.4 0.0 copy-start.7
  105.4 0.0 copy-start.10
  105.4 6.1 %fusion.78 = (f32[1024]{0:T(1024)S(1)}, f32[1024,1024]{1,0:T(8,128)S(1)}) fusion(bf16[4,1024]{1,0:T(4,128)(2,1)S(1)} %collective-permute-done.1, bf16[1024,1024]{1,0:T(8,128)(2,1)S(1)} %multiply_convert_fusion.3, f32[1024]{0:T(1024)S(1)} %bitcast.64, f32[1024]{0:T(1024)S(1)} %bitcast.66, f32[1024]{0:T(1024)S(1)} %bitcast.52, f32[1024]{0:T(1024)S(1)} %bitcast.54, ...), kind=kLoop, calls=%fused_computation.155 | loop fusion | flops 53476352 | bytes 6348800 | tf_op jit(solution)/shard_map/reduce_sum | solution.py:23
  111.5 0.6 multiply_reduce_fusion.2
  112.1 0.0 copy-done
  112.1 0.0 copy-done.7
  112.1 0.0 copy-done.10
  112.1 4.5 %multiply_reduce_fusion = (f32[1024]{0:T(1024)S(1)}, f32[1024]{0:T(1024)S(1)}, f32[1024]{0:T(1024)S(1)}, bf16[1024,1024]{1,0:T(8,128)(2,1)S(1)}, f32[1024,1024]{1,0:T(8,128)S(1)}) fusion(f32[1024,1024]{1,0:T(8,128)S(1)} %get-tuple-element.35, f32[1024]{0:T(1024)S(1)} %add_rsqrt_fusion, f32[1024]{0:T(1024)S(1)} %broadcast_multiply_fusion.4, ...), kind=kOutput, calls=%fused_computation.93 | convolution fusion | flops 2168452096 | bytes 14705664 | tf_op jit(solution)/shard_map/dot_general | solution.py:43
  116.6 0.0 copy-start.13
  116.6 9.8 %fusion.30 = (f32[1024]{0:T(1024)S(1)}, f32[1024]{0:T(1024)S(1)}, f32[1024]{0:T(1024)S(1)}, f32[1024]{0:T(1024)S(1)}, f32[1024]{0:T(1024)S(1)}, /*index=5*/f32[1...) fusion(bf16[4,1024]{1,0:T(4,128)(2,1)S(1)} %collective-permute-done.1, ...), kind=kLoop, calls=%fused_computation.58 | loop fusion | flops 60808192 | bytes 14753792 | tf_op jit(solution)/shard_map/reduce_sum | solution.py:110
  126.4 1.3 collective-permute-start.2
  127.7 4.0 %collective-permute-start.3 = (f32[4,1024]{1,0:T(4,128)S(1)}, f32[4,1024]{1,0:T(4,128)S(1)}, u32[]{:S(2)}, u32[]{:S(2)}) collective-permute-start(f32[4,1024]{1,0:T(4,128)S(1)} %get-tuple-element.38), channel_id=1, source_target_pairs={{0,1},{1,2},{2,3},{3,4},{4,5},{5,6},{6,7},{7,8},{8,9},{9,10},{10,1... | collective-permute-start | bytes 49160 | tf_op jit(solution)/shard_map/ppermute | solution.py:16
  131.7 0.0 copy-done.13
  131.7 4.4 %fusion.73 = f32[1024,1024]{1,0:T(8,128)} fusion(bf16[1024,1024]{1,0:T(8,128)(2,1)S(1)} %get-tuple-element.36, bf16[1,1024,1024]{2,1,0:T(8,128)(2,1)S(1)} %copy-done.7, pred[1024]{0:T(1024)(128)(4,1)S(1)} %broadcast_compare_fusion), kind=kOutput, calls=%fused_computation.153 | convolution fusion | flops 2148532224 | bytes 8389632 | tf_op jit(solution)/shard_map/dot_general | solution.py:37
  136.1 0.0 collective-permute-done.2
  136.1 0.0 collective-permute-done.3
  136.1 9.1 %multiply_convert_fusion.1 = (bf16[1024,1024]{1,0:T(8,128)(2,1)}, f32[1024,1024]{1,0:T(8,128)S(1)}) fusion(f32[1024,2048]{1,0:T(8,128)S(1)} %fusion.75, f32[1024]{0:T(1024)S(1)} %fusion.70, f32[1024,1024]{1,0:T(8,128)S(1)} %get-tuple-element.31, f32[4,1024]{1,0:T(4,128)S(1)} %collective-permute-done.3, f32[1024]{0:T(1024)S(1)} %bitcast.65, ...), kind=kLoop, calls=%fused_computation.95 | loop fusion | flops 32505856 | bytes 14753792 | tf_op jit(solution)/shard_map/convert
  145.2 0.0 copy-start.3
  145.2 1.7 multiply_convert_fusion
  146.9 0.0 copy-start.5
  146.9 1.3 copy-done.5
  148.3 0.0 copy-done.3
  148.3 8.4 %fusion.59 = f32[1024,2048]{1,0:T(8,128)} fusion(bf16[1024,1024]{1,0:T(8,128)(2,1)S(1)} %multiply_convert_fusion, bf16[1024,1024]{1,0:T(8,128)(2,1)S(1)} %copy-done.3, f32[1024]{0:T(1024)S(1)} %copy-done.11, f32[1024]{0:T(1024)S(1)} %add_rsqrt_fusion.1, f32[1024]{0:T(1024)S(1)} %broadcast_multiply_fusion.5, bf16[1024,1024]{1,0:T(8,128)(2,1)S(1)} %copy-done.1, ...), kind=kOutput, calls=%fused_computation.112 | convolution fusion | flops 4309647360 | bytes 14693376 | tf_op jit(solution)/shard_map/dot_general | solution.py:37
  156.7 0.0 all-reduce.4.cloned.1.call-update
  156.7 0.1 stack.39
  156.8 0.0 copy-start.4
  156.8 0.0 copy-start.6
  156.8 0.0 copy-start.12
  156.8 6.1 %fusion.67 = bf16[1,1024,1024]{2,1,0:T(8,128)(2,1)} fusion(f32[1024]{0:T(1024)S(1)} %fusion.70, bf16[1024,1024]{1,0:T(8,128)(2,1)} %copy-done.13, bf16[1024,1024]{1,0:T(8,128)(2,1)S(1)} %copy-done, bf16[1024,1024]{1,0:T(8,128)(2,1)} %gather_fusion, pred[1024]{0:T(1024)(128)(4,1)S(1)} %compare_and_fusion), kind=kOutput, calls=%fused_computation.120 | convolution fusion | flops 2152726528 | bytes 8393728 | tf_op jit(solution)/shard_map/dot_general | solution.py:98
  162.9 0.0 copy-done.2
  162.9 0.0 copy-done.4
  162.9 0.0 copy-done.6
  162.9 0.0 copy-done.12
  162.9 7.2 %fusion.12 = (f32[1024]{0:T(1024)S(1)}, f32[1024]{0:T(1024)S(1)}, f32[1024]{0:T(1024)S(1)}, f32[1024,1024]{1,0:T(8,128)}) fusion(f32[1024]{0:T(1024)S(1)} %add_rsqrt_fusion.1, f32[1024]{0:T(1024)S(1)} %broadcast_multiply_fusion.5, bf16[1024,1024]{1,0:T(8,128)(2,1)S(1)} %copy-done.2, pred[1024]{0:T(1024)(128)(4,1)S(1)} %compare_and_fusion, ...), kind=kOutput, calls=%fused_computation.40 | convolution fusion | flops 4313838592 | bytes 14705664 | tf_op jit(solution)/shard_map/dot_general | solution.py:43
  170.1 77.8 %all-reduce = (f32[9,1024]{1,0:T(8,128)}, f32[1024]{0:T(1024)}, f32[1024]{0:T(1024)}) all-reduce(f32[9,1024]{1,0:T(8,128)S(1)} %stack.39, f32[1024]{0:T(1024)S(1)} %get-tuple-element.9, f32[1024]{0:T(1024)S(1)} %get-tuple-element.7), channel_id=1, replica_groups=mesh['rec'=8,'tm'=16] {'rec','tm'}, use_global_device_ids=true, to_apply=%region_23.24 | all-reduce | flops 11264 | bytes 90112 | tf_op jit(solution)/shard_map/psum | solution.py:130
  247.9 5.5 %fusion.68 = bf16[1,1024,1024]{2,1,0:T(8,128)(2,1)} fusion(f32[1024,1024]{1,0:T(8,128)} %get-tuple-element.51, f32[1024]{0:T(1024)S(1)} %broadcast_multiply_fusion, f32[1024]{0:T(1024)S(1)} %broadcast_multiply_fusion.1, f32[1024]{0:T(1024)S(1)} %copy-done.11, f32[1024]{0:T(1024)S(1)} %add_rsqrt_fusion.1, f32[1024]{0:T(1024)S(1)} %broadcast_multiply_fusion.5, ...), kind=kLoop, calls=%fused_computation.121 | loop fusion | flops 13631488 | bytes 10508288 | tf_op jit(solution)/shard_map/broadcast_in_dim | solution.py:137
  253.4 85.7 %all-reduce.4.cloned.1.call-done = (f32[1024,2048]{1,0:T(8,128)}, f32[1024,1024]{1,0:T(8,128)}) async-done(((f32[1024,2048]{1,0:T(8,128)}, f32[1024,1024]{1,0:T(8,128)}), (f32[1024,2048]{1,0:T(8,128)}, f32[1024,1024]{1,0:T(8,128)})) %all-reduce.4.cloned.1.call-update) | async-done | bytes 12582928 | tf_op jit(solution)/shard_map/psum | solution.py:132
  339.1 1.9 constant_dynamic-slice_fusion
  340.9 1.7 constant_dynamic-slice_fusion.1
  (21 shorter events, 0.2 us)
Async XLA Ops:
  7.2 104.9 %copy-start = (bf16[1024,1024]{1,0:T(8,128)(2,1)S(1)}, bf16[1024,1024]{1,0:T(8,128)(2,1)}, u32[]{:S(2)}) copy-start(bf16[1024,1024]{1,0:T(8,128)(2,1)} %param.17) | copy-start | bytes 6291460
  7.2 9.4 %copy-start.9 = (s32[1,16,16]{2,1,0:T(8,128)S(1)}, s32[1,16,16]{2,1,0:T(8,128)}, u32[]{:S(2)}) copy-start(s32[1,16,16]{2,1,0:T(8,128)} %param.10) | copy-start | bytes 3076
  7.2 10.0 %copy-start.8 = (f32[9,1024]{1,0:T(8,128)S(1)}, f32[9,1024]{1,0:T(8,128)}, u32[]{:S(2)}) copy-start(f32[9,1024]{1,0:T(8,128)} %param.15) | copy-start | bytes 110596
  7.2 70.1 %all-to-all-start = ((bf16[16,128,1024]{2,1,0:T(8,128)(2,1)}), bf16[16,128,1024]{2,1,0:T(8,128)(2,1)}, u32[]{:S(2)}, u32[]{:S(2)}) async-start(bf16[16,128,1024]{2,1,0:T(8,128)(2,1)} %bitcast.49), calls=%async_computation | async-start | bytes 8388608 | tf_op jit(solution)/shard_map/all_to_all | solution.py:67
  15.8 323.2 %all-reduce.4.cloned.1.call-start = ((), (), s32[]{:S(2)}) async-start(), calls=%async_computation.1 | async-start | bytes 25165824 | tf_op jit(solution)/shard_map/psum | solution.py:132
  86.1 4.8 %copy-start.1 = (bf16[1024,1024]{1,0:T(8,128)(2,1)S(1)}, bf16[1024,1024]{1,0:T(8,128)(2,1)}, u32[]{:S(2)}) copy-start(bf16[1024,1024]{1,0:T(8,128)(2,1)} %gather_fusion) | copy-start | bytes 6291460
  86.1 4.8 %copy-start.11 = (f32[1024]{0:T(1024)S(1)}, f32[1024]{0:T(1024)}, u32[]{:S(2)}) copy-start(f32[1024]{0:T(1024)} %param.13) | copy-start | bytes 12292
  99.7 2.8 collective-permute-start
  101.0 4.4 %collective-permute-start.1 = (bf16[4,1024]{1,0:T(4,128)(2,1)S(1)}, bf16[4,1024]{1,0:T(4,128)(2,1)S(1)}, u32[]{:S(2)}, u32[]{:S(2)}) collective-permute-start(bf16[4,1024]{1,0:T(4,128)(2,1)S(1)} %get-tuple-element.40), channel_id=1, source_target_pairs={{1,0},{2,1},{3,2},{4,3},{5,4},{6,5},{7,6},{8,7},{9,8},{10,9},{11,1... | collective-permute-start | bytes 24584 | tf_op jit(solution)/shard_map/ppermute | solution.py:17
  105.4 6.7 %copy-start.7 = (bf16[1,1024,1024]{2,1,0:T(8,128)(2,1)S(1)}, bf16[1,1024,1024]{2,1,0:T(8,128)(2,1)}, u32[]{:S(2)}) copy-start(bf16[1,1024,1024]{2,1,0:T(8,128)(2,1)} %param.12) | copy-start | bytes 6291460
  105.4 6.7 %copy-start.10 = (f32[1024]{0:T(1024)S(1)}, f32[1024]{0:T(1024)}, u32[]{:S(2)}) copy-start(f32[1024]{0:T(1024)} %param.16) | copy-start | bytes 12292
  116.6 15.1 %copy-start.13 = (bf16[1024,1024]{1,0:T(8,128)(2,1)}, bf16[1024,1024]{1,0:T(8,128)(2,1)S(1)}, u32[]{:S(2)}) copy-start(bf16[1024,1024]{1,0:T(8,128)(2,1)S(1)} %get-tuple-element.36) | copy-start | bytes 6291460
  126.4 9.7 %collective-permute-start.2 = (f32[4,1024]{1,0:T(4,128)S(1)}, f32[4,1024]{1,0:T(4,128)S(1)}, u32[]{:S(2)}, u32[]{:S(2)}) collective-permute-start(f32[4,1024]{1,0:T(4,128)S(1)} %get-tuple-element.37), channel_id=1, source_target_pairs={{1,0},{2,1},{3,2},{4,3},{5,4},{6,5},{7,6},{8,7},{9,8},{10,9},{11,1... | collective-permute-start | bytes 49160 | tf_op jit(solution)/shard_map/ppermute | solution.py:17
  127.7 8.4 %collective-permute-start.3 = (f32[4,1024]{1,0:T(4,128)S(1)}, f32[4,1024]{1,0:T(4,128)S(1)}, u32[]{:S(2)}, u32[]{:S(2)}) collective-permute-start(f32[4,1024]{1,0:T(4,128)S(1)} %get-tuple-element.38), channel_id=1, source_target_pairs={{0,1},{1,2},{2,3},{3,4},{4,5},{5,6},{6,7},{7,8},{8,9},{9,10},{10,1... | collective-permute-start | bytes 49160 | tf_op jit(solution)/shard_map/ppermute | solution.py:16
  145.2 3.1 copy-start.3
  146.9 1.4 copy-start.5
  156.8 6.1 %copy-start.2 = (bf16[1024,1024]{1,0:T(8,128)(2,1)S(1)}, bf16[1024,1024]{1,0:T(8,128)(2,1)}, u32[]{:S(2)}) copy-start(bf16[1024,1024]{1,0:T(8,128)(2,1)} %gather_fusion) | copy-start | bytes 6291460
  156.8 6.1 %copy-start.4 = (bf16[1024,1024]{1,0:T(8,128)(2,1)S(1)}, bf16[1024,1024]{1,0:T(8,128)(2,1)}, u32[]{:S(2)}) copy-start(bf16[1024,1024]{1,0:T(8,128)(2,1)} %get-tuple-element.32) | copy-start | bytes 6291460
  156.8 6.1 %copy-start.6 = (bf16[1024,1024]{1,0:T(8,128)(2,1)S(1)}, bf16[1024,1024]{1,0:T(8,128)(2,1)}, u32[]{:S(2)}) copy-start(bf16[1024,1024]{1,0:T(8,128)(2,1)} %copy-done.5) | copy-start | bytes 6291460
  156.8 6.1 %copy-start.12 = (bf16[1024,2048]{1,0:T(8,128)(2,1)S(1)}, bf16[1024,2048]{1,0:T(8,128)(2,1)}, u32[]{:S(2)}) copy-start(bf16[1024,2048]{1,0:T(8,128)(2,1)} %param.14) | copy-start | bytes 12582916
Sparse Core Ops, SparseCore 0:
  156.8 182.1 all-reduce.3
where the time goes:
time: 350 us; the launch traced here: 349 us
  waiting for transfers between devices  149 us (43%)
  blocking collectives  77.8 us (22%)
  other arithmetic  39.5 us (11%)
  matrix products  37.8 us (11%)
  starting transfers between devices  16.7 us (5%)
  between operations  15.1 us (4%)
  local copies, waits for them, and re-layouts  13.9 us (4%)
    psum x1, waiting for transfers between devices, per_device(): lax.psum((grad_expand, grad_project), ('rec', 'tm'))  85.7 us
    psum x1, blocking collectives, per_device(): lax.psum((grad_taps, grad_norm_gain, grad_conv_gain), ('rec', 'tm'))  77.8 us
    all_to_all x1, waiting for transfers between devices, per_device(): lax.all_to_all(buckets, 'tm', split_axis=0, concat_axis=0, tiled=True)  60.1 us
    dot_general x2, matrix products, contract_rows(): lax.dot_general(left, right, (((0,), (0,)), ((), ())), preferred_element_...  12.8 us
    dot_general x2, matrix products, contract_cols(): lax.dot_general(left, right, (((1,), (1,)), ((), ())), preferred_element_...  11.7 us
    another operation x4, other arithmetic  11 us
    reduce_sum x1, other arithmetic, per_device(): jnp.sum(grad_depth * glu_rim[kernel_tap:kernel_tap + frames].astype(jnp.f...  9.76 us
    gather x1, local copies, waits for them, and re-layouts, per_device(): sequence = jnp.take(arrived, row_index, axis=0)  8.73 us
  transfers between devices with their start and end apart: 6, of which 3 were waited for; matrix products, arithmetic and copies ran while one was open for 7% of the time, Pallas kernels for 0%

commit v1 on v0

v1 whole, which is shorter than its diff:
```python
import functools

import jax
import jax.numpy as jnp
from jax import lax
from jax.experimental import pallas as pl
from jax.experimental.pallas import tpu as pltpu
from jax.sharding import PartitionSpec as P

EPS = 1e-05
MESH = pl.DeviceIdType.MESH
DMA = pltpu.SemaphoreType.DMA
F32 = jnp.float32
BF16 = jnp.bfloat16
D = 1024
FR = 1024
CAP = 128
KER = 9
HALO = 8
EXT = FR + 2 * HALO
VMEM_LIMIT = 60 * 1024 * 1024


def place():
    rec, tm = lax.axis_index("rec"), lax.axis_index("tm")
    return rec // 2, rec % 2, tm // 4, tm % 4


def device(y, core, x, z):
    return (lax.rem(y + 4, 4) * 2 + core, lax.rem(x + 4, 4) * 4 + lax.rem(z + 4, 4))


def greet(devices):
    barrier = pltpu.get_barrier_semaphore()
    for d in devices:
        pl.semaphore_signal(barrier, inc=1, device_id=d, device_id_type=MESH)
    pl.semaphore_wait(barrier, len(devices))


def contract_rows(left, right):
    return lax.dot_general(left, right, (((0,), (0,)), ((), ())), preferred_element_type=F32)


def contract_cols(left, right):
    return lax.dot_general(left, right, (((1,), (1,)), ((), ())), preferred_element_type=F32)


def row_frames(start, rows):
    row = start + lax.broadcasted_iota(jnp.int32, (rows, 1), 0)
    return jnp.where(row < FR + HALO, row, row - EXT)


OFFSETS = [(dx, dz) for dx in range(4) for dz in range(4) if (dx, dz) != (0, 0)]
SIGNED = (0, 1, None, -1)


def routes():
    out = []
    for dx, dz in OFFSETS:
        for half in (0, 1):
            sign = 1 - 2 * half
            step_x, step_z = (sign if d == 2 else SIGNED[d] for d in (dx, dz))
            along_x = [(step_x, 0)] * (0 if dx == 0 else 2 if dx == 2 else 1)
            along_z = [(0, step_z)] * (0 if dz == 0 else 2 if dz == 2 else 1)
            hops = along_x + along_z if half == 0 else along_z + along_x
            out.append(((dx, dz), half, hops))
    return sorted(out, key=lambda r: -len(r[2]))


ROUTES = routes()
N_HOPS = sum(len(r[2]) for r in ROUTES)
N_RELAY = sum(len(r[2]) - 1 for r in ROUTES)
PIECE = CAP // 2


def regroup_kernel(
    loader, cot, counts, length, w_project, seq, gsw,
    arrived, relay, cot_v, edge, wp_v, send, recv, local, edge_sem,
):
    y, core, x, z = place()
    me = x * 4 + z
    greet([device(y, core, x + dx, z + dz) for dx, dz in OFFSETS])

    hop_id, slot = {}, {}
    for i, (_, _, hops) in enumerate(ROUTES):
        for k in range(len(hops)):
            hop_id[i, k] = len(hop_id)
            if k < len(hops) - 1:
                slot[i, k] = len(slot)
    copies = {}

    def launch(i, k, src):
        (dx, dz), half, hops = ROUTES[i]
        gone_x, gone_z = (sum(h[a] for h in hops[:k]) for a in (0, 1))
        if k == len(hops) - 1:
            origin = lax.rem(x - gone_x + 4, 4) * 4 + lax.rem(z - gone_z + 4, 4)
            dst = arrived.at[pl.ds(origin * CAP + half * PIECE, PIECE)]
        else:
            dst = relay.at[pl.ds(slot[i, k] * PIECE, PIECE)]
        j = hop_id[i, k]
        copies[i, k] = pltpu.make_async_remote_copy(
            src, dst, send.at[j], recv.at[j],
            device_id=device(y, core, x + hops[k][0], z + hops[k][1]), device_id_type=MESH,
        )
        copies[i, k].start()

    for i, ((dx, dz), half, _) in enumerate(ROUTES):
        to = lax.rem(x + dx, 4) * 4 + lax.rem(z + dz, 4)
        launch(i, 0, loader.at[pl.ds(to * CAP + half * PIECE, PIECE)])
    own = pltpu.make_async_copy(loader.at[pl.ds(me * CAP, CAP)], arrived.at[pl.ds(me * CAP, CAP)], local.at[0])
    own.start()
    left = device(y, core, lax.rem(me + 15, 16) // 4, lax.rem(me + 15, 16) % 4)
    right = device(y, core, lax.rem(me + 1, 16) // 4, lax.rem(me + 1, 16) % 4)
    get_cot = pltpu.make_async_copy(cot, cot_v, local.at[1])
    get_wp = pltpu.make_async_copy(w_project, wp_v, local.at[2])
    get_cot.start()
    get_wp.start()
    first = pltpu.make_async_remote_copy(
        cot.at[pl.ds(0, 16)], edge.at[0], edge_sem.at[0], edge_sem.at[1], device_id=left, device_id_type=MESH)
    last = pltpu.make_async_remote_copy(
        cot.at[pl.ds(FR - 16, 16)], edge.at[1], edge_sem.at[2], edge_sem.at[3], device_id=right, device_id_type=MESH)
    first.start()
    last.start()
    live = length[0] - me * FR
    get_cot.wait()
    get_wp.wait()

    @pl.loop(0, 4)
    def _(k):
        r0 = pl.multiple_of(k * 256, 256)
        frame = r0 + lax.broadcasted_iota(jnp.int32, (256, 1), 0)
        tile = cot_v[pl.ds(r0, 256)]
        tile = jnp.where(frame < live, tile, jnp.zeros_like(tile))
        gsw[pl.ds(r0, 256)] = contract_cols(tile, wp_v[...])

    first.wait()
    last.wait()
    rim = jnp.concatenate([edge[0].astype(F32)[:HALO], edge[1].astype(F32)[16 - HALO :]], axis=0)
    frame = row_frames(FR, 2 * HALO)
    rim = jnp.where((frame < live) & (frame + me * FR >= 0), rim, 0.0).astype(BF16)
    gsw[pl.ds(FR, 2 * HALO)] = contract_cols(rim, wp_v[...])

    for k in range(1, 4):
        for i, (_, _, hops) in enumerate(ROUTES):
            if k < len(hops):
                copies[i, k - 1].wait_recv()
                launch(i, k, relay.at[pl.ds(slot[i, k - 1] * PIECE, PIECE)])
    own.wait()
    for (i, k), copy in copies.items():
        copy.wait_send()
        if k == len(ROUTES[i][2]) - 1:
            copy.wait_recv()

    begin = jnp.int32(0)
    places = []
    lane = lax.broadcasted_iota(jnp.int32, (1, CAP), 1)
    for j in range(16):
        count = counts[j, me]
        places.append(jnp.where(lane < count, begin + lane, -1))
        begin = begin + count
    places = jnp.concatenate(places, axis=1)

    @pl.loop(0, 4)
    def _(k):
        r0 = pl.multiple_of(k * 256, 256)
        frame = r0 + lax.broadcasted_iota(jnp.int32, (256, 1), 0)
        pick = jnp.where(frame == places, 1.0, 0.0).astype(BF16)
        seq[pl.ds(r0, 256)] = jnp.dot(pick, arrived[...], preferred_element_type=F32)

    first = pltpu.make_async_remote_copy(
        seq.at[pl.ds(0, HALO)], seq.at[pl.ds(FR, HALO)], edge_sem.at[4], edge_sem.at[5], device_id=left, device_id_type=MESH)
    last = pltpu.make_async_remote_copy(
        seq.at[pl.ds(FR - HALO, HALO)], seq.at[pl.ds(FR + HALO, HALO)], edge_sem.at[6], edge_sem.at[7], device_id=right, device_id_type=MESH)
    first.start()
    last.start()
    first.wait()
    last.wait()


def regroup(loader, cot, counts, length, w_project):
    any_space = pl.BlockSpec(memory_space=pl.ANY)
    vmem = pl.BlockSpec(memory_space=pltpu.VMEM)
    smem = pl.BlockSpec(memory_space=pltpu.SMEM)
    return pl.pallas_call(
        regroup_kernel,
        out_shape=[jax.ShapeDtypeStruct((EXT, D), F32), jax.ShapeDtypeStruct((EXT, D), F32)],
        in_specs=[any_space, any_space, smem, smem, any_space],
        out_specs=[vmem, vmem],
        scratch_shapes=[
            pltpu.VMEM((16 * CAP, D), BF16),
            pltpu.VMEM((N_RELAY * PIECE, D), BF16),
            pltpu.VMEM((FR, D), BF16),
            pltpu.VMEM((2, 16, D), BF16),
            pltpu.VMEM((D, D), BF16),
            DMA((N_HOPS,)),
            DMA((N_HOPS,)),
            DMA((3,)),
            DMA((8,)),
        ],
        compiler_params=pltpu.CompilerParams(collective_id=0, has_side_effects=True, vmem_limit_bytes=VMEM_LIMIT),
    )(loader, cot, counts, length, w_project)


def mean(values):
    return jnp.mean(values, axis=-1, keepdims=True)


def normalize(values):
    center = values - mean(values)
    inverse = lax.rsqrt(mean(center * center) + EPS)
    return center * inverse, inverse


def norm_back(grad, normed, inverse):
    return inverse * (grad - mean(grad) - normed * mean(grad * normed))


def fold(values):
    return jnp.sum(values.reshape(-1, 8, values.shape[-1]), axis=0)


T1 = 208
RT = 64
CC = 256


def shard_kernel(
    length, seq, gsw, cot, norm_gain, w_expand, taps, conv_gain, w_project,
    layer_out, grad_in, weights, small,
    glu, lin, gate, scaled, dgrad, swished, gout, gexp, dw, tapsum, gainsum,
):
    me = lax.axis_index("tm")
    live = length[0] - me * FR

    @pl.loop(0, EXT // T1)
    def _(k):
        r0 = pl.multiple_of(k * T1, 16)
        normed, _ = normalize(seq[pl.ds(r0, T1)])
        s = (normed * norm_gain[...]).astype(BF16)
        scaled[pl.ds(r0, T1)] = s
        frame = row_frames(r0, T1)
        valid = (frame < live) & (frame + me * FR >= 0)
        for c in range(0, D, 512):
            a = jnp.dot(s, w_expand[:, c : c + 512], preferred_element_type=F32)
            b = jax.nn.sigmoid(jnp.dot(s, w_expand[:, D + c : D + c + 512], preferred_element_type=F32))
            lin[pl.ds(r0, T1), c : c + 512] = a
            gate[pl.ds(r0, T1), c : c + 512] = b
            glu[pl.ds(r0 + 16, T1), c : c + 512] = jnp.where(valid, a * b, 0.0).astype(BF16).astype(F32)

    glu[pl.ds(8, 8)] = glu[pl.ds(16 + FR + HALO, 8)]
    glu[pl.ds(0, 8)] = jnp.zeros((8, D), F32)
    gainsum[...] = jnp.zeros_like(gainsum)
    tapsum[...] = jnp.zeros_like(tapsum)

    def middle(at, rows, gs_at):
        for c in range(0, D, CC):
            wide = glu[pl.ds(at - 8, rows + 16), c : c + CC]
            acc = taps[0:1, c : c + CC] * wide[4 : 4 + rows]
            for t in range(1, KER):
                acc = acc + taps[t : t + 1, c : c + CC] * wide[4 + t : 4 + t + rows]
            dw[pl.ds(0, rows), c : c + CC] = acc
        normed, inverse = normalize(dw[pl.ds(0, rows)])
        sc = normed * conv_gain[...]
        sig = jax.nn.sigmoid(sc)
        gsc = gsw[pl.ds(gs_at, rows)] * sig * (1.0 + sc * (1.0 - sig))
        dgrad[pl.ds(at, rows)] = norm_back(gsc * conv_gain[...], normed, inverse)
        return sc * sig, gsc * normed

    @pl.loop(0, FR // RT)
    def _(k):
        r0 = pl.multiple_of(k * RT, RT)
        sw, gc = middle(pl.multiple_of(r0 + 16, 16), RT, r0)
        swished[pl.ds(r0, RT)] = sw.astype(BF16)
        gainsum[0] += fold(gc)

    middle(16 + FR, HALO, FR)
    middle(8 + 0, HALO, FR + HALO)

    @pl.loop(0, 4)
    def _(k):
        r0 = pl.multiple_of(k * 256, 256)
        frame = r0 + lax.broadcasted_iota(jnp.int32, (256, 1), 0)
        tile = cot[pl.ds(r0, 256)]
        gout[pl.ds(r0, 256)] = jnp.where(frame < live, tile, jnp.zeros_like(tile))
        projected = jnp.dot(swished[pl.ds(r0, 256)], w_project[...], preferred_element_type=F32)
        layer_out[pl.ds(r0, 256)] = jnp.where(frame < live, seq[pl.ds(r0, 256)] + projected, 0.0).astype(BF16)

    @pl.loop(0, 4)
    def _(k):
        c0 = pl.multiple_of(k * 256, 256)
        weights[pl.ds(c0, 256), 2 * D :] = contract_rows(swished[:, pl.ds(c0, 256)], gout[...]).astype(BF16)

    @pl.loop(0, FR // RT)
    def _(k):
        r0 = pl.multiple_of(k * RT, RT)
        frame = r0 + lax.broadcasted_iota(jnp.int32, (RT, 1), 0)
        for c in range(0, D, CC):
            wide = dgrad[pl.ds(pl.multiple_of(r0 + 8, 8), RT + 16), c : c + CC]
            mid = glu[pl.ds(pl.multiple_of(r0 + 16, 16), RT), c : c + CC]
            acc = jnp.zeros((RT, CC), F32)
            for t in range(KER):
                shifted = wide[12 - t : 12 - t + RT]
                acc = acc + taps[t : t + 1, c : c + CC] * shifted
                tapsum[t, :, c : c + CC] += fold(mid * shifted)
            a = lin[pl.ds(r0, RT), c : c + CC]
            b = gate[pl.ds(r0, RT), c : c + CC]
            gg = jnp.where(frame < live, acc, 0.0) * b
            gexp[pl.ds(r0, RT), c : c + CC] = gg.astype(BF16)
            gexp[pl.ds(r0, RT), D + c : D + c + CC] = (gg * a * (1.0 - b)).astype(BF16)

    @pl.loop(0, 4)
    def _(k):
        c0 = pl.multiple_of(k * 256, 256)
        for c in range(0, 2 * D, 1024):
            weights[pl.ds(c0, 256), c : c + 1024] = contract_rows(
                scaled[pl.ds(0, FR), pl.ds(c0, 256)], gexp[:, c : c + 1024]).astype(BF16)

    @pl.loop(0, 4)
    def _(k):
        r0 = pl.multiple_of(k * 256, 256)
        grad_scaled = contract_cols(gexp[pl.ds(r0, 256)], w_expand[...])
        normed, inverse = normalize(seq[pl.ds(r0, 256)])
        gainsum[1] += fold(grad_scaled * normed)
        grad_in[pl.ds(r0, 256)] = (
            gout[pl.ds(r0, 256)].astype(F32) + norm_back(grad_scaled * norm_gain[...], normed, inverse)
        ).astype(BF16)

    small[...] = jnp.zeros_like(small)
    for t in range(KER):
        small[t : t + 1] = jnp.sum(tapsum[t], axis=0, keepdims=True)
    small[9:10] = jnp.sum(gainsum[1], axis=0, keepdims=True)
    small[10:11] = jnp.sum(gainsum[0], axis=0, keepdims=True)


def shard_work(length, seq, gsw, cot, norm_gain, w_expand, taps, conv_gain, w_project):
    vmem = pl.BlockSpec(memory_space=pltpu.VMEM)
    smem = pl.BlockSpec(memory_space=pltpu.SMEM)
    rows = FR + 2 * 16
    return pl.pallas_call(
        shard_kernel,
        out_shape=[
            jax.ShapeDtypeStruct((FR, D), BF16),
            jax.ShapeDtypeStruct((FR, D), BF16),
            jax.ShapeDtypeStruct((D, 3 * D), BF16),
            jax.ShapeDtypeStruct((16, D), F32),
        ],
        in_specs=[smem] + [vmem] * 8,
        out_specs=[vmem] * 4,
        scratch_shapes=[
            pltpu.VMEM((rows, D), F32),
            pltpu.VMEM((EXT, D), F32),
            pltpu.VMEM((EXT, D), F32),
            pltpu.VMEM((EXT, D), BF16),
            pltpu.VMEM((rows, D), F32),
            pltpu.VMEM((FR, D), BF16),
            pltpu.VMEM((FR, D), BF16),
            pltpu.VMEM((FR, 2 * D), BF16),
            pltpu.VMEM((RT, D), F32),
            pltpu.VMEM((KER, 8, D), F32),
            pltpu.VMEM((2, 8, D), F32),
        ],
        compiler_params=pltpu.CompilerParams(vmem_limit_bytes=VMEM_LIMIT),
    )(length, seq, gsw, cot, norm_gain, w_expand, taps, conv_gain, w_project)


ORDERS = (("x", "z", "y"), ("z", "y", "x"), ("y", "x", "z"))
COLS = 512
HALF = COLS // 2


def sum_kernel(
    weights, small, out_expand, out_project, out_small,
    mine, part, hop1, hop2, final, pair_small, ring_small, full_small,
    load_sem, pair_sem, hop_send, hop_recv, fin_sem, sm_sem,
):
    y, core, x, z = place()
    pos = {"x": x, "y": y, "z": z}

    def along(axis, by):
        at = dict(pos)
        at[axis] = pos[axis] + by
        return device(at["y"], core, at["x"], at["z"])

    partner = device(y, 1 - core, x, z)
    greet([partner] + [along(a, b) for a in "xyz" for b in (1, 2, 3)])

    loads, pairs = [], []
    for p in range(3):
        away = pl.multiple_of((1 - core) * 1536 + p * COLS, COLS)
        c = pltpu.make_async_remote_copy(
            weights.at[:, :, :, :, pl.ds(away, COLS)], part.at[p], pair_sem.at[0, p], pair_sem.at[1, p],
            device_id=partner, device_id_type=MESH)
        c.start()
        pairs.append(c)
        here = pl.multiple_of(core * 1536 + p * COLS, COLS)
        c = pltpu.make_async_copy(weights.at[:, :, :, :, pl.ds(here, COLS)], mine.at[p], load_sem.at[p])
        c.start()
        loads.append(c)
    away = pl.multiple_of((1 - core) * 512, 512)
    here = pl.multiple_of(core * 512, 512)
    small_pair = pltpu.make_async_remote_copy(
        small.at[:, pl.ds(away, 512)], pair_small, sm_sem.at[0, 0], sm_sem.at[1, 0], device_id=partner, device_id_type=MESH)
    small_pair.start()
    done = []

    def view(p, s, c, cols):
        index = {"x": slice(None), "z": slice(None), "y": slice(None)}
        for a in ORDERS[p][:s]:
            index[a] = pos[a]
        index[ORDERS[p][s]] = lax.rem(c + 4, 4)
        return (p, index["x"], index["z"], index["y"], slice(None), cols)

    LO, HI = pl.ds(0, HALF), pl.ds(HALF, HALF)

    def buffer(ref, p, s, k):
        return ref[s].at[p, k]

    def start(p, s, n, src, dst, by):
        c = pltpu.make_async_remote_copy(
            src, dst, hop_send.at[p, s, n], hop_recv.at[p, s, n],
            device_id=along(ORDERS[p][s], by), device_id_type=MESH)
        c.start()
        return c

    def small_stage(s, axis, value):
        buf = ring_small.at[s]
        buf[pos[axis]] = value
        out = []
        for by in (1, 2, 3):
            c = pltpu.make_async_remote_copy(
                buf.at[pos[axis]], buf.at[pos[axis]], sm_sem.at[0, 1 + 3 * s + by - 1], sm_sem.at[1, 1 + 3 * s + by - 1],
                device_id=along(axis, by), device_id_type=MESH)
            c.start()
            out.append(c)
        return out

    def small_sum(s, copies):
        for c in copies:
            c.wait()
        b = ring_small.at[s]
        return (b[0] + b[1]) + (b[2] + b[3])

    small_value = small_copies = None
    stage = {}
    for s in range(3):
        for p in range(3):
            if s == 0:
                loads[p].wait()
                pairs[p].wait_recv()

                @pl.loop(0, 4)
                def _(i):
                    @pl.loop(0, 4)
                    def _(j):
                        part[p, i, j] = (part[p, i, j].astype(F32) + mine[p, i, j].astype(F32)).astype(BF16)

            m = pos[ORDERS[p][s]]
            stage[p] = [
                start(p, s, 0, part.at[view(p, s, m + 2, LO)], buffer(hop1, p, s, 0), 1),
                start(p, s, 1, part.at[view(p, s, m + 2, HI)], buffer(hop1, p, s, 1), -1),
                start(p, s, 2, part.at[view(p, s, m + 1, HI)], buffer(hop2, p, s, 0), 1),
                start(p, s, 3, part.at[view(p, s, m - 1, LO)], buffer(hop2, p, s, 1), -1),
            ]
        if s == 0:
            small_pair.wait()
            small_value = small[:, pl.ds(here, 512)] + pair_small[...]
        small_copies = small_stage(s, "xzy"[s], small_value)
        for p in range(3):
            m = pos[ORDERS[p][s]]
            stage[p][0].wait_recv()
            at = view(p, s, m + 1, LO)
            part[at] = (part[at].astype(F32) + hop1[s][p, 0].astype(F32)).astype(BF16)
            stage[p].append(start(p, s, 4, part.at[at], buffer(hop2, p, s, 2), 1))
            stage[p][1].wait_recv()
            at = view(p, s, m - 1, HI)
            part[at] = (part[at].astype(F32) + hop1[s][p, 1].astype(F32)).astype(BF16)
            stage[p].append(start(p, s, 5, part.at[at], buffer(hop2, p, s, 3), -1))
        small_value = small_sum(s, small_copies)
        for p in range(3):
            m = pos[ORDERS[p][s]]
            for c in stage[p][2:]:
                c.wait_recv()
            low, high = view(p, s, m, LO), view(p, s, m, HI)
            sum_low = part[low].astype(F32) + hop2[s][p, 2].astype(F32) + hop2[s][p, 1].astype(F32)
            sum_high = part[high].astype(F32) + hop2[s][p, 0].astype(F32) + hop2[s][p, 3].astype(F32)
            if s < 2:
                part[low] = sum_low.astype(BF16)
                part[high] = sum_high.astype(BF16)
            else:
                final[core, y, :, p * COLS : p * COLS + HALF] = sum_low.astype(BF16)
                final[core, y, :, p * COLS + HALF : (p + 1) * COLS] = sum_high.astype(BF16)
            done += stage[p]

    gather = []
    for by in (1, 2, 3):
        c = pltpu.make_async_remote_copy(
            final.at[core, y], final.at[core, y], fin_sem.at[0, by - 1], fin_sem.at[1, by - 1],
            device_id=along("y", by), device_id_type=MESH)
        c.start()
        gather.append(c)
    full_small[core] = small_value
    small_last = pltpu.make_async_remote_copy(
        full_small.at[core], full_small.at[core], sm_sem.at[0, 10], sm_sem.at[1, 10], device_id=partner, device_id_type=MESH)
    small_last.start()
    for c in gather:
        c.wait_recv()
    last = pltpu.make_async_remote_copy(
        final.at[core], final.at[core], fin_sem.at[0, 3], fin_sem.at[1, 3], device_id=partner, device_id_type=MESH)
    last.start()
    small_last.wait()
    out_small[:, 0:512] = full_small[0]
    out_small[:, 512:1024] = full_small[1]
    last.wait()
    for k in range(4):
        rows = slice(k * 16, k * 16 + 16)
        out_expand[rows, 0:1536] = final[0, k].astype(F32)
        out_expand[rows, 1536:2048] = final[1, k][:, 0:512].astype(F32)
        out_project[rows, :] = final[1, k][:, 512:1536].astype(F32)
    for c in gather + pairs + done:
        c.wait_send()


def sum_all(weights, small):
    any_space = pl.BlockSpec(memory_space=pl.ANY)
    vmem = pl.BlockSpec(memory_space=pltpu.VMEM)

    def hop_shapes(n):
        return [pltpu.VMEM((3, n) + (4,) * (2 - s) + (16, HALF), BF16) for s in range(3)]

    return pl.pallas_call(
        lambda w, s, oe, op, os, mine, part, a0, a1, a2, b0, b1, b2, *rest: sum_kernel(
            w, s, oe, op, os, mine, part, (a0, a1, a2), (b0, b1, b2), *rest),
        out_shape=[
            jax.ShapeDtypeStruct((D // 16, 2 * D), F32),
            jax.ShapeDtypeStruct((D // 16, D), F32),
            jax.ShapeDtypeStruct((16, D), F32),
        ],
        in_specs=[any_space, vmem],
        out_specs=[vmem] * 3,
        scratch_shapes=[
            pltpu.VMEM((3, 4, 4, 4, 16, COLS), BF16),
            pltpu.VMEM((3, 4, 4, 4, 16, COLS), BF16),
            *hop_shapes(2),
            *hop_shapes(4),
            pltpu.VMEM((2, 4, 16, 3 * COLS), BF16),
            pltpu.VMEM((16, 512), F32),
            pltpu.VMEM((3, 4, 16, 512), F32),
            pltpu.VMEM((2, 16, 512), F32),
            DMA((3,)),
            DMA((2, 3)),
            DMA((3, 3, 6)),
            DMA((3, 3, 6)),
            DMA((2, 4)),
            DMA((2, 11)),
        ],
        compiler_params=pltpu.CompilerParams(collective_id=1, has_side_effects=True, vmem_limit_bytes=VMEM_LIMIT),
    )(weights.reshape(4, 4, 4, 16, 3 * D), small)


def per_device(
    loader_rows, frame_counts, lengths, cotangent, norm_gain, w_expand, conv_taps, conv_gain, w_project,
):
    seq, gsw = regroup(loader_rows[0], cotangent[0], frame_counts[0], lengths, w_project)
    layer_out, grad_in, weights, small = shard_work(
        lengths, seq, gsw, cotangent[0], norm_gain[None], w_expand, conv_taps, conv_gain[None], w_project)
    expand, project, small = sum_all(weights, small)
    return layer_out[None], grad_in[None], expand, project, small[:KER], small[9], small[10]


def solution(mesh):
    return jax.shard_map(
        per_device,
        mesh=mesh,
        in_specs=(
            P("rec", "tm", None), P("rec", None, None), P("rec"), P("rec", "tm", None),
            P(), P(), P(), P(), P(),
        ),
        out_specs=(
            P("rec", "tm", None), P("rec", "tm", None), P("tm", None), P("tm", None), P(), P(), P(),
        ),
        check_vma=False,
    )
```

time: 350 us -> 187 us (0.53)
  Pallas kernels: 0 us -> 179 us
  waiting for transfers between devices: 149 us -> 0 us
  blocking collectives: 77.8 us -> 0 us
  other arithmetic: 39.5 us -> 0 us
  matrix products: 37.8 us -> 0 us
  starting transfers between devices: 16.7 us -> 0 us
  between operations: 15.1 us -> 1.3 us
  local copies, waits for them, and re-layouts: 13.9 us -> 6.45 us
    pallas_call x0 -> x3, Pallas kernels: none -> 179 us  [the longest x1 75.7 us: regroup(): pl.pallas_call(regroup_kernel, out_shape=[jax.ShapeDtypeStruct((EXT, D),...]
    psum x1 -> x0, waiting for transfers between devices: 85.7 us -> none  [per_device(): lax.psum((grad_expand, grad_project), ('rec', 'tm'))]
    psum x1 -> x0, blocking collectives: 77.8 us -> none  [per_device(): lax.psum((grad_taps, grad_norm_gain, grad_conv_gain), ('rec', 'tm'))]
    all_to_all x1 -> x0, waiting for transfers between devices: 60.1 us -> none  [per_device(): lax.all_to_all(buckets, 'tm', split_axis=0, concat_axis=0, tiled=True)]
    dot_general x6 -> x0, matrix products: 37.8 us -> none  [the longest x2 12.8 us: contract_rows(): lax.dot_general(left, right, (((0,), (0,)), ((), ())), preferred_element_...]
    reduce_sum x8 -> x0, other arithmetic: 21.4 us -> none  [the longest x1 9.76 us: per_device(): jnp.sum(grad_depth * glu_rim[kernel_tap:kernel_tap + frames].astype(jnp.f...]
    another operation x4 -> x0, other arithmetic: 11 us -> none
    gather x1 -> x0, local copies, waits for them, and re-layouts: 8.73 us -> none  [per_device(): sequence = jnp.take(arrived, row_index, axis=0)]
  transfers between devices with their start and end apart: 6 -> 0, of which waited for: 3 -> 0; matrix products, arithmetic and copies ran while one was open for 7% -> 0% of each run, Pallas kernels for 0% -> 0%
where the time goes in v1:
time: 187 us
  Pallas kernels  179 us (96%)
  local copies, waits for them, and re-layouts  6.45 us (3%)
    pallas_call x1, Pallas kernels, regroup(): pl.pallas_call(regroup_kernel, out_shape=[jax.ShapeDtypeStruct((EXT, D),...  75.7 us
    pallas_call x1, Pallas kernels, shard_work(): pl.pallas_call(shard_kernel, out_shape=[jax.ShapeDtypeStruct((FR, D), BF1...  57 us
    pallas_call x1, Pallas kernels, sum_all(): pl.pallas_call(lambda w, s, oe, op, os, mine, part, a0, a1, a2, b0, b1, b...  46.1 us
    unnamed x3, local copies, waits for them, and re-layouts  5.01 us

profile of v1, /device:TPU:1, one launch (start us, length us, event | category | flops | bytes accessed | tf_op | source)
XLA Modules:
  0.0 186.7 jit_solution(13387568767184429714)
XLA Ops:
  1.3 75.7 %shard_map.144 = (f32[1040,1024]{1,0:T(8,128)}, f32[1040,1024]{1,0:T(8,128)}) custom-call(bf16[2048,1024]{1,0:T(8,128)(2,1)} %bitcast.14, bf16[1024,1024]{1,0:T(8,128)(2,1)} %bitcast.11, s32[16,16]{1,0:T(8,128)} %bitcast.16, s32[1]{0:T(128)S(6)} %copy.19.length, bf16[1024,1024]{1,0:T(8,128)(2,1)} %w_project.3), custom_call_target="tpu_custom_call" | custom-call | tf_op jit(solution)/shard_map/pallas_call | solution.py:184
  77.0 57.0 %shard_map.145 = (bf16[1024,1024]{1,0:T(8,128)(2,1)}, bf16[1024,1024]{1,0:T(8,128)(2,1)}, bf16[1024,3072]{1,0:T(8,128)(2,1)}, f32[16,1024]{1,0:T(8,128)}) custom-call(s32[1]{0:T(128)S(6)} %copy.19.length, f32[1040,1024]{1,0:T(8,128)} %get-tuple-element.16.seq, f32[1040,1024]{1,0:T(8,128)} %get-tuple-element.17.gsw, bf16[1024,1024]{1,0:T(8,128)(2,1)} %bitcast.12, ...), custom_call_target="tpu_custom_call" | custom-call | tf_op jit(solution)/shard_map/pallas_call | solution.py:339
  134.1 46.1 %shard_map.146 = (f32[64,2048]{1,0:T(8,128)}, f32[64,1024]{1,0:T(8,128)}, f32[16,1024]{1,0:T(8,128)}) custom-call(bf16[4,4,4,16,3072]{4,3,2,1,0:T(8,128)(2,1)} %bitcast.13, f32[16,1024]{1,0:T(8,128)} %get-tuple-element.21.s), custom_call_target="tpu_custom_call" | custom-call | tf_op jit(solution)/shard_map/pallas_call | solution.py:530
  180.2 1.4 fusion
  181.7 1.9 %copy.20 = f32[64,2048]{1,0:T(8,128)} copy(f32[64,2048]{1,0:T(8,128)} %get-tuple-element.36) | data formatting | bytes 1048576
  183.5 1.7 copy.21
  185.2 1.5 copy.22

commit v2 on v0

v2 whole, which is shorter than its diff:
```python
import functools

import jax
import jax.numpy as jnp
from jax import lax
from jax.experimental import pallas as pl
from jax.experimental.pallas import tpu as pltpu
from jax.sharding import PartitionSpec as P

EPS = 1e-05
MESH = pl.DeviceIdType.MESH
DMA = pltpu.SemaphoreType.DMA
F32 = jnp.float32
BF16 = jnp.bfloat16
D = 1024
FR = 1024
CAP = 128
KER = 9
HALO = 8
EXT = FR + 2 * HALO
VMEM_LIMIT = 61 * 1024 * 1024


def place():
    rec, tm = lax.axis_index("rec"), lax.axis_index("tm")
    return rec // 2, rec % 2, tm // 4, tm % 4


def device(y, core, x, z):
    return (lax.rem(y + 4, 4) * 2 + core, lax.rem(x + 4, 4) * 4 + lax.rem(z + 4, 4))


def greet(devices):
    barrier = pltpu.get_barrier_semaphore()
    for d in devices:
        pl.semaphore_signal(barrier, inc=1, device_id=d, device_id_type=MESH)
    pl.semaphore_wait(barrier, len(devices))


def contract_rows(left, right):
    return lax.dot_general(left, right, (((0,), (0,)), ((), ())), preferred_element_type=F32)


def contract_cols(left, right):
    return lax.dot_general(left, right, (((1,), (1,)), ((), ())), preferred_element_type=F32)


def row_frames(start, rows):
    row = start + lax.broadcasted_iota(jnp.int32, (rows, 1), 0)
    return jnp.where(row < FR + HALO, row, row - EXT)


OFFSETS = [(dx, dz) for dx in range(4) for dz in range(4) if (dx, dz) != (0, 0)]
SIGNED = (0, 1, None, -1)


def routes():
    out = []
    for dx, dz in OFFSETS:
        for half in (0, 1):
            sign_x = (1 - 2 * half) * (-1 if dz == 3 else 1)
            sign_z = (1 - 2 * half) * (-1 if dx == 1 else 1)
            step_x = sign_x if dx == 2 else SIGNED[dx]
            step_z = sign_z if dz == 2 else SIGNED[dz]
            along_x = [(step_x, 0)] * (0 if dx == 0 else 2 if dx == 2 else 1)
            along_z = [(0, step_z)] * (0 if dz == 0 else 2 if dz == 2 else 1)
            hops = along_x + along_z if half == 0 else along_z + along_x
            out.append(((dx, dz), half, hops))
    return sorted(out, key=lambda r: -len(r[2]))


ROUTES = routes()
N_HOPS = sum(len(r[2]) for r in ROUTES)
N_RELAY = sum(len(r[2]) - 1 for r in ROUTES)
PIECE = CAP // 2


def mean(values):
    return jnp.mean(values, axis=-1, keepdims=True)


def normalize(values):
    center = values - mean(values)
    inverse = lax.rsqrt(mean(center * center) + EPS)
    return center * inverse, inverse


def norm_back(grad, normed, inverse):
    return inverse * (grad - mean(grad) - normed * mean(grad * normed))


def fold(values):
    return jnp.sum(values.reshape(-1, 8, values.shape[-1]), axis=0)


T1 = 208
RC = 80
RB = 64
RT = 64
CC = 128


ORDERS = (("y", "x", "z"), ("x", "z", "y"), ("z", "y", "x"))
COLS = 512
HALF = COLS // 2
LO, HI = pl.ds(0, HALF), pl.ds(HALF, HALF)


def kernel(
    loader, cot, counts, length, norm_gain, w_expand, taps, conv_gain, w_project,
    layer_out, grad_in, relay, out_sum, out_small,
    arrived, cotv, edge, wp, we, seq, gsw, glu, dgrad, lin, gate, scaled, swished, gainsum, small,
    away, pair, part, hop1_0, hop1_1, hop1_2, hop2_0, hop2_1, hop2_2, final, pair_small, ring_small, full_small,
    send, recv, local, edge_sem, pair_sem, hop_send, hop_recv, fin_sem, sm_sem,
):
    hop1, hop2 = (hop1_0, hop1_1, hop1_2), (hop2_0, hop2_1, hop2_2)
    y, core, x, z = place()
    pos = {"x": x, "y": y, "z": z}
    me = x * 4 + z
    live = length[0] - me * FR
    partner = device(y, 1 - core, x, z)

    def along(axis, by):
        at = dict(pos)
        at[axis] = pos[axis] + by
        return device(at["y"], core, at["x"], at["z"])

    greet([device(y, core, x + dx, z + dz) for dx, dz in OFFSETS] + [partner] + [along("y", b) for b in (1, 2, 3)])

    hop_id, slot = {}, {}
    for i, (_, _, hops) in enumerate(ROUTES):
        for k in range(len(hops)):
            hop_id[i, k] = len(hop_id)
            if k < len(hops) - 1:
                slot[i, k] = len(slot)
    copies = {}

    def launch(i, k, src):
        _, half, hops = ROUTES[i]
        gone_x, gone_z = (sum(h[a] for h in hops[:k]) for a in (0, 1))
        if k == len(hops) - 1:
            origin = lax.rem(x - gone_x + 4, 4) * 4 + lax.rem(z - gone_z + 4, 4)
            dst = arrived.at[pl.ds(origin * CAP + half * PIECE, PIECE)]
        else:
            dst = relay.at[pl.ds(slot[i, k] * PIECE, PIECE)]
        j = hop_id[i, k]
        copies[i, k] = pltpu.make_async_remote_copy(
            src, dst, send.at[j], recv.at[j],
            device_id=device(y, core, x + hops[k][0], z + hops[k][1]), device_id_type=MESH,
        )
        copies[i, k].start()

    before, after = lax.rem(me + 15, 16), lax.rem(me + 1, 16)
    left = device(y, core, before // 4, lax.rem(before, 4))
    right = device(y, core, after // 4, lax.rem(after, 4))
    first = pltpu.make_async_remote_copy(
        cot.at[pl.ds(0, 16)], edge.at[0], edge_sem.at[0], edge_sem.at[1], device_id=left, device_id_type=MESH)
    last = pltpu.make_async_remote_copy(
        cot.at[pl.ds(FR - 16, 16)], edge.at[1], edge_sem.at[2], edge_sem.at[3], device_id=right, device_id_type=MESH)
    first.start()
    last.start()
    for i, ((dx, dz), half, _) in enumerate(ROUTES):
        to = lax.rem(x + dx, 4) * 4 + lax.rem(z + dz, 4)
        launch(i, 0, loader.at[pl.ds(to * CAP + half * PIECE, PIECE)])
    own = pltpu.make_async_copy(loader.at[pl.ds(me * CAP, CAP)], arrived.at[pl.ds(me * CAP, CAP)], local.at[0])
    get_cot = pltpu.make_async_copy(cot, cotv, local.at[1])
    get_wp = pltpu.make_async_copy(w_project, wp, local.at[2])
    get_we = pltpu.make_async_copy(w_expand, we, local.at[3])
    for c in (get_cot, get_wp, own, get_we):
        c.start()
    get_cot.wait()
    get_wp.wait()

    @pl.loop(0, 4)
    def _(k):
        r0 = pl.multiple_of(k * 256, 256)
        frame = r0 + lax.broadcasted_iota(jnp.int32, (256, 1), 0)
        tile = cotv[pl.ds(r0, 256)]
        tile = jnp.where(frame < live, tile, jnp.zeros_like(tile))
        cotv[pl.ds(r0, 256)] = tile
        gsw[pl.ds(r0, 256)] = contract_cols(tile, wp[...])

    gainsum[...] = jnp.zeros_like(gainsum)
    small[...] = jnp.zeros_like(small)

    for k in range(1, 4):
        for i, (_, _, hops) in enumerate(ROUTES):
            if k < len(hops):
                copies[i, k - 1].wait_recv()
                launch(i, k, relay.at[pl.ds(slot[i, k - 1] * PIECE, PIECE)])

    first.wait()
    last.wait()
    rim = jnp.concatenate([edge[0].astype(F32)[:HALO], edge[1].astype(F32)[16 - HALO :]], axis=0)
    frame = row_frames(FR, 2 * HALO)
    rim = jnp.where((frame < live) & (frame + me * FR >= 0), rim, 0.0).astype(BF16)
    gsw[pl.ds(FR, 2 * HALO)] = contract_cols(rim, wp[...])
    column = [counts[j, me] for j in range(16)]
    lane = lax.broadcasted_iota(jnp.int32, (1, CAP), 1)

    def collect(offsets, fresh):
        origins, places = [], []
        for dx, dz in offsets:
            origin = lax.rem(x - dx + 4, 4) * 4 + lax.rem(z - dz + 4, 4)
            begin = count = jnp.int32(0)
            for j in range(16):
                begin = begin + jnp.where(j < origin, column[j], 0)
                count = count + jnp.where(j == origin, column[j], 0)
            origins.append(origin)
            places.append(jnp.where(lane < count, begin + lane, -1))
        places = jnp.concatenate(places, axis=1)

        @pl.loop(0, 4)
        def _(k):
            r0 = pl.multiple_of(k * 256, 256)
            frame = r0 + lax.broadcasted_iota(jnp.int32, (256, 1), 0)
            pick = jnp.where(frame == places, 1.0, 0.0).astype(BF16)
            rows = jnp.concatenate([arrived[pl.ds(pl.multiple_of(o * CAP, CAP), CAP)] for o in origins], axis=0)
            got = jnp.dot(pick, rows, preferred_element_type=F32)
            seq[pl.ds(r0, 256)] = got if fresh else seq[pl.ds(r0, 256)] + got

    own.wait()
    for n, some in enumerate(((3, 4), (2,), (1,))):
        here = []
        for i, (offset, _, hops) in enumerate(ROUTES):
            if len(hops) in some:
                copies[i, len(hops) - 1].wait_recv()
                if offset not in here:
                    here.append(offset)
        collect(here + [(0, 0)] * (n == 0), n == 0)

    first = pltpu.make_async_remote_copy(
        seq.at[pl.ds(0, HALO)], seq.at[pl.ds(FR, HALO)], edge_sem.at[4], edge_sem.at[5], device_id=left, device_id_type=MESH)
    last = pltpu.make_async_remote_copy(
        seq.at[pl.ds(FR - HALO, HALO)], seq.at[pl.ds(FR + HALO, HALO)], edge_sem.at[6], edge_sem.at[7], device_id=right, device_id_type=MESH)
    first.start()
    last.start()
    get_we.wait()

    @pl.loop(0, EXT // T1)
    def _(k):
        @pl.when(k == EXT // T1 - 1)
        def _():
            first.wait()
            last.wait()

        r0 = pl.multiple_of(k * T1, 16)
        normed, _ = normalize(seq[pl.ds(r0, T1)])
        scaled[pl.ds(r0, T1)] = (normed * norm_gain[...]).astype(BF16)
        frame = row_frames(r0, T1)
        valid = (frame < live) & (frame + me * FR >= 0)

        @pl.loop(0, 2)
        def _(h):
            c = pl.multiple_of(h * 512, 512)
            s = scaled[pl.ds(r0, T1)]
            a = jnp.dot(s, we[:, pl.ds(c, 512)], preferred_element_type=F32)
            b = jax.nn.sigmoid(jnp.dot(s, we[:, pl.ds(D + c, 512)], preferred_element_type=F32))
            lin[pl.ds(r0, T1), pl.ds(c, 512)] = a
            gate[pl.ds(r0, T1), pl.ds(c, 512)] = b
            glu[pl.ds(pl.multiple_of(r0 + 16, 16), T1), pl.ds(c, 512)] = jnp.where(valid, a * b, 0.0).astype(BF16).astype(F32)

    glu[pl.ds(8, 8)] = glu[pl.ds(16 + FR + HALO, 8)]
    glu[pl.ds(0, 8)] = jnp.zeros((8, D), F32)

    @pl.loop(0, D // CC)
    def _(n):
        c = pl.ds(pl.multiple_of(n * CC, CC), CC)
        tap = [jnp.broadcast_to(taps[t : t + 1, c], (8, CC)) for t in range(KER)]

        @pl.loop(0, EXT // RC)
        def _(k):
            r0 = pl.multiple_of(k * RC, 16)
            wide = glu[pl.ds(r0, RC + 16), c]
            acc = None
            for t in range(KER):
                term = (wide[4 + t : 4 + t + RC].reshape(RC // 8, 8, CC) * tap[t]).reshape(RC, CC)
                acc = term if acc is None else acc + term
            dgrad[pl.ds(pl.multiple_of(r0 + 8, 8), RC), c] = acc

    def middle(depth, gs):
        normed, inverse = normalize(depth)
        sc = normed * conv_gain[...]
        sig = jax.nn.sigmoid(sc)
        sw = sc * sig
        gsc = gs * (sig + sw * (1.0 - sig))
        return norm_back(gsc * conv_gain[...], normed, inverse), sw, gsc * normed

    @pl.loop(0, FR // RT)
    def _(k):
        r0 = pl.multiple_of(k * RT, RT)
        at = pl.ds(pl.multiple_of(r0 + 16, 16), RT)
        gd, sw, gc = middle(dgrad[at], gsw[pl.ds(r0, RT)])
        dgrad[at] = gd
        swished[pl.ds(r0, RT)] = sw.astype(BF16)
        gainsum[0] += fold(gc)

    gd, _, _ = middle(
        jnp.concatenate([dgrad[8:16], dgrad[FR + 16 : FR + 24]], axis=0),
        jnp.concatenate([gsw[FR + HALO : EXT], gsw[FR : FR + HALO]], axis=0))
    dgrad[8:16] = gd[:8]
    dgrad[FR + 16 : FR + 24] = gd[8:]

    def view(p, s, c, cols):
        index = {"x": slice(None), "z": slice(None), "y": slice(None)}
        for a in ORDERS[p][:s]:
            index[a] = pos[a]
        index[ORDERS[p][s]] = lax.rem(c + 4, 4)
        return (p, index["x"], index["z"], index["y"], slice(None), cols)

    flying, pairs, done = {}, {}, []

    def pair_start(p):
        pairs[p] = pltpu.make_async_remote_copy(
            away.at[p], pair.at[p], pair_sem.at[0, p], pair_sem.at[1, p], device_id=partner, device_id_type=MESH)
        pairs[p].start()

    def pair_finish(p):
        pairs[p].wait_recv()

        @pl.loop(0, 16)
        def _(i):
            a, b = i // 4, lax.rem(i, 4)
            part[p, a, b] = (part[p, a, b].astype(F32) + pair[p, a, b].astype(F32)).astype(BF16)

    def step(p, s, n, at, dst, by):
        c = pltpu.make_async_remote_copy(
            part.at[at], dst, hop_send.at[p, s, n], hop_recv.at[p, s, n],
            device_id=along(ORDERS[p][s], by), device_id_type=MESH)
        c.start()
        flying[p, s].append(c)
        done.append(c)

    def ring_start(p, s):
        m = pos[ORDERS[p][s]]
        flying[p, s] = []
        step(p, s, 0, view(p, s, m + 2, LO), hop1[s].at[p, 0], 1)
        step(p, s, 1, view(p, s, m + 2, HI), hop1[s].at[p, 1], -1)
        step(p, s, 2, view(p, s, m + 1, HI), hop2[s].at[p, 0], 1)
        step(p, s, 3, view(p, s, m - 1, LO), hop2[s].at[p, 1], -1)

    def ring_middle(p, s):
        m = pos[ORDERS[p][s]]
        for n, (by, cols) in enumerate(((1, LO), (-1, HI))):
            flying[p, s][n].wait_recv()
            at = view(p, s, m + by, cols)
            part[at] = (part[at].astype(F32) + hop1[s][p, n].astype(F32)).astype(BF16)
            step(p, s, 4 + n, at, hop2[s].at[p, 2 + n], by)

    def ring_end(p, s):
        m = pos[ORDERS[p][s]]
        for c in flying[p, s][2:]:
            c.wait_recv()
        low, high = view(p, s, m, LO), view(p, s, m, HI)
        sum_low = part[low].astype(F32) + hop2[s][p, 2].astype(F32) + hop2[s][p, 1].astype(F32)
        sum_high = part[high].astype(F32) + hop2[s][p, 0].astype(F32) + hop2[s][p, 3].astype(F32)
        if s < 2:
            part[low] = sum_low.astype(BF16)
            part[high] = sum_high.astype(BF16)
        else:
            final[core, y, :, p * COLS : p * COLS + HALF] = sum_low.astype(BF16)
            final[core, y, :, p * COLS + HALF : (p + 1) * COLS] = sum_high.astype(BF16)

    small_flying = {}

    def small_start(s, value):
        axis = "xzy"[s]
        buf = ring_small.at[s]
        buf[pos[axis]] = value
        small_flying[s] = []
        for by in (1, 2, 3):
            c = pltpu.make_async_remote_copy(
                buf.at[pos[axis]], buf.at[pos[axis]], sm_sem.at[0, 3 * s + by], sm_sem.at[1, 3 * s + by],
                device_id=along(axis, by), device_id_type=MESH)
            c.start()
            small_flying[s].append(c)

    def small_end(s):
        for c in small_flying[s]:
            c.wait()
        b = ring_small.at[s]
        return (b[0] + b[1]) + (b[2] + b[3])

    def project_grad(dst, half):
        @pl.loop(0, 4)
        def _(k):
            value = contract_rows(
                swished[:, pl.ds(pl.multiple_of(k * 256, 256), 256)], cotv[:, pl.ds(pl.multiple_of(half * 512, 512), 512)])
            dst[0, k] = value.astype(BF16).reshape(4, 4, 16, COLS)

    project_grad(away, 1 - core)
    pair_start(0)
    project_grad(part, core)

    @pl.loop(0, 4)
    def _(k):
        r0 = pl.multiple_of(k * 256, 256)
        frame = r0 + lax.broadcasted_iota(jnp.int32, (256, 1), 0)
        projected = jnp.dot(swished[pl.ds(r0, 256)], wp[...], preferred_element_type=F32)
        swished[pl.ds(r0, 256)] = jnp.where(frame < live, seq[pl.ds(r0, 256)] + projected, 0.0).astype(BF16)

    put_out = pltpu.make_async_copy(swished, layer_out, local.at[4])
    put_out.start()
    pair_finish(0)
    ring_start(0, 0)

    def conv_back(lo, hi):
        @pl.loop(lo, hi)
        def _(n):
            c = pl.ds(pl.multiple_of(n * CC, CC), CC)
            tap = [jnp.broadcast_to(taps[t : t + 1, c], (8, CC)) for t in range(KER)]

            def rows(k, sums):
                r0 = pl.multiple_of(k * RB, RB)
                frame = r0 + lax.broadcasted_iota(jnp.int32, (RB, 1), 0)
                wide = dgrad[pl.ds(pl.multiple_of(r0 + 8, 8), RB + 16), c]
                mid = glu[pl.ds(pl.multiple_of(r0 + 16, 16), RB), c]
                acc, new = None, []
                for t in range(KER):
                    shifted = wide[12 - t : 12 - t + RB]
                    term = (shifted.reshape(RB // 8, 8, CC) * tap[t]).reshape(RB, CC)
                    acc = term if acc is None else acc + term
                    new.append(sums[t] + fold(mid * shifted))
                a = lin[pl.ds(r0, RB), c]
                b = gate[pl.ds(r0, RB), c]
                gg = jnp.where(frame < live, acc, 0.0) * b
                arrived[pl.ds(r0, RB), c] = gg.astype(BF16)
                arrived[pl.ds(pl.multiple_of(FR + r0, RB), RB), c] = (gg * a * (1.0 - b)).astype(BF16)
                return tuple(new)

            sums = lax.fori_loop(0, FR // RB, rows, tuple(jnp.zeros((8, CC), F32) for _ in range(KER)))
            for t in range(KER):
                small[t : t + 1, c] = jnp.sum(sums[t], axis=0, keepdims=True)

    conv_back(0, 4)
    ring_middle(0, 0)
    conv_back(4, 8)

    def expand_grad(dst, half):
        @pl.loop(0, 4)
        def _(k):
            value = contract_rows(
                scaled[pl.ds(0, FR), pl.ds(pl.multiple_of(k * 256, 256), 256)],
                arrived[pl.ds(pl.multiple_of(half * FR, FR), FR)]).astype(BF16)
            dst[1, k] = value[:, :COLS].reshape(4, 4, 16, COLS)
            dst[2, k] = value[:, COLS:].reshape(4, 4, 16, COLS)

    expand_grad(away, 1 - core)
    pair_start(1)
    pair_start(2)
    ring_end(0, 0)
    ring_start(0, 1)
    expand_grad(part, core)
    for p in (1, 2):
        pair_finish(p)
        ring_start(p, 0)
    ring_middle(0, 1)

    def input_grad(lo, hi):
        @pl.loop(lo, hi)
        def _(k):
            r0 = pl.multiple_of(k * 256, 256)
            grad_scaled = contract_cols(arrived[pl.ds(r0, 256)], we[:, :D]) + contract_cols(
                arrived[pl.ds(pl.multiple_of(FR + r0, 256), 256)], we[:, D:])
            normed, inverse = normalize(seq[pl.ds(r0, 256)])
            gainsum[1] += fold(grad_scaled * normed)
            cotv[pl.ds(r0, 256)] = (
                cotv[pl.ds(r0, 256)].astype(F32) + norm_back(grad_scaled * norm_gain[...], normed, inverse)
            ).astype(BF16)

    input_grad(0, 2)
    for p in (1, 2):
        ring_middle(p, 0)
    input_grad(2, 4)
    put_grad = pltpu.make_async_copy(cotv, grad_in, local.at[5])
    put_grad.start()
    small[9:10] = jnp.sum(gainsum[1], axis=0, keepdims=True)
    small[10:11] = jnp.sum(gainsum[0], axis=0, keepdims=True)
    there = pl.multiple_of((1 - core) * 512, 512)
    here = pl.multiple_of(core * 512, 512)
    small_pair = pltpu.make_async_remote_copy(
        small.at[:, pl.ds(there, 512)], pair_small, sm_sem.at[0, 0], sm_sem.at[1, 0], device_id=partner, device_id_type=MESH)
    small_pair.start()
    for p in (1, 2):
        ring_end(p, 0)
        ring_start(p, 1)
    ring_end(0, 1)
    ring_start(0, 2)
    small_pair.wait()
    small_start(0, small[:, pl.ds(here, 512)] + pair_small[...])
    for p in (1, 2):
        ring_middle(p, 1)
    ring_middle(0, 2)
    small_start(1, small_end(0))
    for p in (1, 2):
        ring_end(p, 1)
        ring_start(p, 2)
    ring_end(0, 2)
    for p in (1, 2):
        ring_middle(p, 2)
    small_start(2, small_end(1))
    for p in (1, 2):
        ring_end(p, 2)

    gather = []
    for by in (1, 2, 3):
        c = pltpu.make_async_remote_copy(
            final.at[core, y], final.at[core, y], fin_sem.at[0, by - 1], fin_sem.at[1, by - 1],
            device_id=along("y", by), device_id_type=MESH)
        c.start()
        gather.append(c)
    full_small[core] = small_end(2)
    small_last = pltpu.make_async_remote_copy(
        full_small.at[core], full_small.at[core], sm_sem.at[0, 10], sm_sem.at[1, 10], device_id=partner, device_id_type=MESH)
    small_last.start()
    for c in gather:
        c.wait_recv()
    final_last = pltpu.make_async_remote_copy(
        final.at[core], final.at[core], fin_sem.at[0, 3], fin_sem.at[1, 3], device_id=partner, device_id_type=MESH)
    final_last.start()
    for c in list(copies.values()) + gather + list(pairs.values()) + done:
        c.wait_send()
    put_out.wait()
    put_grad.wait()
    small_last.wait()
    out_small[:, 0:512] = full_small[0]
    out_small[:, 512:1024] = full_small[1]
    final_last.wait()
    out_sum[...] = final[...]


def finish_kernel(layer_in, grad_src, sums, small, layer_out, grad_in, expand, project, taps, norm_gain, conv_gain):
    layer_out[0] = layer_in[...]
    grad_in[0] = grad_src[...]

    @pl.when(pl.program_id(0) == 0)
    def _():
        for k in range(4):
            for c in range(2):
                rows = sums[c, k].astype(F32)
                project[k * 16 : k * 16 + 16, c * 512 : (c + 1) * 512] = rows[:, :512]
                expand[k * 16 : k * 16 + 16, c * 1024 : (c + 1) * 1024] = rows[:, 512:]
        taps[...] = small[0:KER]
        norm_gain[...] = small[9:10]
        conv_gain[...] = small[10:11]


def per_device(
    loader_rows, frame_counts, lengths, cotangent, norm_gain, w_expand, conv_taps, conv_gain, w_project,
):
    any_space = pl.BlockSpec(memory_space=pl.ANY)
    vmem = pl.BlockSpec(memory_space=pltpu.VMEM)
    smem = pl.BlockSpec(memory_space=pltpu.SMEM)

    def hop_shapes(n):
        return [pltpu.VMEM((3, n) + (4,) * (2 - s) + (16, HALF), BF16) for s in range(3)]

    layer_out, grad_in, _, sums, small = pl.pallas_call(
        kernel,
        out_shape=[
            jax.ShapeDtypeStruct((FR, D), BF16),
            jax.ShapeDtypeStruct((FR, D), BF16),
            jax.ShapeDtypeStruct((N_RELAY * PIECE, D), BF16),
            jax.ShapeDtypeStruct((2, 4, 16, 3 * COLS), BF16),
            jax.ShapeDtypeStruct((16, D), F32),
        ],
        in_specs=[any_space, any_space, smem, smem, vmem, any_space, vmem, vmem, any_space],
        out_specs=[any_space] * 3 + [vmem] * 2,
        scratch_shapes=[
            pltpu.VMEM((16 * CAP, D), BF16),
            pltpu.VMEM((FR, D), BF16),
            pltpu.VMEM((2, 16, D), BF16),
            pltpu.VMEM((D, D), BF16),
            pltpu.VMEM((D, 2 * D), BF16),
            pltpu.VMEM((EXT, D), F32),
            pltpu.VMEM((EXT, D), F32),
            pltpu.VMEM((FR + 32, D), F32),
            pltpu.VMEM((FR + 32, D), F32),
            pltpu.VMEM((EXT, D), F32),
            pltpu.VMEM((EXT, D), F32),
            pltpu.VMEM((EXT, D), BF16),
            pltpu.VMEM((FR, D), BF16),
            pltpu.VMEM((2, 8, D), F32),
            pltpu.VMEM((16, D), F32),
            pltpu.VMEM((3, 4, 4, 4, 16, COLS), BF16),
            pltpu.VMEM((3, 4, 4, 4, 16, COLS), BF16),
            pltpu.VMEM((3, 4, 4, 4, 16, COLS), BF16),
            *hop_shapes(2),
            *hop_shapes(4),
            pltpu.VMEM((2, 4, 16, 3 * COLS), BF16),
            pltpu.VMEM((16, 512), F32),
            pltpu.VMEM((3, 4, 16, 512), F32),
            pltpu.VMEM((2, 16, 512), F32),
            DMA((N_HOPS,)),
            DMA((N_HOPS,)),
            DMA((6,)),
            DMA((8,)),
            DMA((2, 3)),
            DMA((3, 3, 6)),
            DMA((3, 3, 6)),
            DMA((2, 4)),
            DMA((2, 11)),
        ],
        compiler_params=pltpu.CompilerParams(collective_id=0, has_side_effects=True, vmem_limit_bytes=VMEM_LIMIT),
    )(
        loader_rows[0], cotangent[0], frame_counts[0], lengths, norm_gain[None], w_expand, conv_taps, conv_gain[None],
        w_project,
    )
    layer_out, grad_in, expand, project, taps, norm_gain, conv_gain = pl.pallas_call(
        finish_kernel,
        out_shape=[
            jax.ShapeDtypeStruct((1, FR, D), BF16),
            jax.ShapeDtypeStruct((1, FR, D), BF16),
            jax.ShapeDtypeStruct((D // 16, 2 * D), F32),
            jax.ShapeDtypeStruct((D // 16, D), F32),
            jax.ShapeDtypeStruct((KER, D), F32),
            jax.ShapeDtypeStruct((1, D), F32),
            jax.ShapeDtypeStruct((1, D), F32),
        ],
        grid=(4,),
        in_specs=[pl.BlockSpec((FR // 4, D), lambda i: (i, 0))] * 2 + [vmem] * 2,
        out_specs=[pl.BlockSpec((1, FR // 4, D), lambda i: (0, i, 0))] * 2 + [vmem] * 5,
    )(layer_out, grad_in, sums, small)
    return layer_out, grad_in, expand, project, taps, norm_gain[0], conv_gain[0]


def solution(mesh):
    return jax.shard_map(
        per_device,
        mesh=mesh,
        in_specs=(
            P("rec", "tm", None), P("rec", None, None), P("rec"), P("rec", "tm", None),
            P(), P(), P(), P(), P(),
        ),
        out_specs=(
            P("rec", "tm", None), P("rec", "tm", None), P("tm", None), P("tm", None), P(), P(), P(),
        ),
        check_vma=False,
    )
```

time: 350 us -> 150 us (0.43)
  Pallas kernels: 0 us -> 149 us
  waiting for transfers between devices: 149 us -> 0 us
  blocking collectives: 77.8 us -> 0 us
  other arithmetic: 39.5 us -> 0 us
  matrix products: 37.8 us -> 0 us
  starting transfers between devices: 16.7 us -> 0 us
  local copies, waits for them, and re-layouts: 13.9 us -> 0 us
  between operations: 15.1 us -> 1.29 us
    pallas_call x0 -> x2, Pallas kernels: none -> 149 us  [the longest x1 144 us: per_device(): pl.pallas_call(kernel, out_shape=[jax.ShapeDtypeStruct((FR, D), BF16), ja...]
    psum x1 -> x0, waiting for transfers between devices: 85.7 us -> none  [per_device(): lax.psum((grad_expand, grad_project), ('rec', 'tm'))]
    psum x1 -> x0, blocking collectives: 77.8 us -> none  [per_device(): lax.psum((grad_taps, grad_norm_gain, grad_conv_gain), ('rec', 'tm'))]
    all_to_all x1 -> x0, waiting for transfers between devices: 60.1 us -> none  [per_device(): lax.all_to_all(buckets, 'tm', split_axis=0, concat_axis=0, tiled=True)]
    dot_general x6 -> x0, matrix products: 37.8 us -> none  [the longest x2 12.8 us: contract_rows(): lax.dot_general(left, right, (((0,), (0,)), ((), ())), preferred_element_...]
    reduce_sum x8 -> x0, other arithmetic: 21.4 us -> none  [the longest x1 9.76 us: per_device(): jnp.sum(grad_depth * glu_rim[kernel_tap:kernel_tap + frames].astype(jnp.f...]
    another operation x4 -> x0, other arithmetic: 11 us -> none
    gather x1 -> x0, local copies, waits for them, and re-layouts: 8.73 us -> none  [per_device(): sequence = jnp.take(arrived, row_index, axis=0)]
  transfers between devices with their start and end apart: 6 -> 0, of which waited for: 3 -> 0; matrix products, arithmetic and copies ran while one was open for 7% -> 0% of each run, Pallas kernels for 0% -> 0%
where the time goes in v2:
time: 150 us
  Pallas kernels  149 us (99%)
    pallas_call x1, Pallas kernels, per_device(): pl.pallas_call(kernel, out_shape=[jax.ShapeDtypeStruct((FR, D), BF16), ja...  144 us
    pallas_call x1, Pallas kernels, per_device(): pl.pallas_call(finish_kernel, out_shape=[jax.ShapeDtypeStruct((1, FR, D),...  5.14 us

profile of v2, /device:TPU:1, one launch (start us, length us, event | category | flops | bytes accessed | tf_op | source)
XLA Modules:
  0.0 150.0 jit_solution(14104189271191769565)
XLA Ops:
  1.3 143.5 %shard_map.144 = (bf16[1024,1024]{1,0:T(8,128)(2,1)}, bf16[1024,1024]{1,0:T(8,128)(2,1)}, bf16[2176,1024]{1,0:T(8,128)(2,1)}, bf16[2,4,16,1536]{3,2,1,0:T(8,128)(2,1)}, f32[16,1024]{1,0:T(8,128)}) custom-call(bf16[2048,1024]{1,0:T(8,128)(2,1)} %bitcast.7, bf16[1024,1024]{1,0:T(8,128)(2,1)} %bitcast.8, s32[16,16]{1,0:T(8,128)} %bitcast.9, s32[1]{0:T(128)S(6)} %copy.16.length, ...), custom_call_target="tpu_custom_call" | custom-call | tf_op jit(solution)/shard_map/pallas_call | solution.py:558
  144.8 5.1 %shard_map.145 = (bf16[1,1024,1024]{2,1,0:T(8,128)(2,1)}, bf16[1,1024,1024]{2,1,0:T(8,128)(2,1)}, f32[64,2048]{1,0:T(8,128)}, f32[64,1024]{1,0:T(8,128)}, f32[9,...) custom-call(bf16[1024,1024]{1,0:T(8,128)(2,1)} %get-tuple-element.18.layer_in, ...), custom_call_target="tpu_custom_call" | custom-call | tf_op jit(solution)/shard_map/pallas_call | solution.py:609

commit v3 on v2

--- a/solution.py
+++ b/solution.py
@@ -79,14 +79,21 @@
     return jnp.mean(values, axis=-1, keepdims=True)
 
 
-def normalize(values):
-    center = values - mean(values)
-    inverse = lax.rsqrt(mean(center * center) + EPS)
-    return center * inverse, inverse
-
-
-def norm_back(grad, normed, inverse):
-    return inverse * (grad - mean(grad) - normed * mean(grad * normed))
+def lanes(n):
+    return slice(n * CC, (n + 1) * CC)
+
+
+def spread(values):
+    return jnp.broadcast_to(mean(values) * (CC / D), values.shape)
+
+
+def moments(load):
+    center = spread(sum(load(n) for n in range(D // CC)))
+    square = None
+    for n in range(D // CC):
+        off = load(n) - center
+        square = off * off if square is None else square + off * off
+    return center, lax.rsqrt(spread(square) + EPS)
 
 
 def fold(values):
@@ -94,26 +101,25 @@
 
 
 T1 = 208
-RC = 80
-RB = 64
+RM = 128
+RC = 208
+RB = 128
 RT = 64
 CC = 128
 
 
-ORDERS = (("y", "x", "z"), ("x", "z", "y"), ("z", "y", "x"))
-COLS = 512
-HALF = COLS // 2
-LO, HI = pl.ds(0, HALF), pl.ds(HALF, HALF)
+ORDERS = (("z", "x"), ("x", "z"), ("z", "x"))
+WIDTH = (512, 768, 256)
+START = (0, 512, 1280)
 
 
 def kernel(
     loader, cot, counts, length, norm_gain, w_expand, taps, conv_gain, w_project,
     layer_out, grad_in, relay, out_sum, out_small,
-    arrived, cotv, edge, wp, we, seq, gsw, glu, dgrad, lin, gate, scaled, swished, gainsum, small,
-    away, pair, part, hop1_0, hop1_1, hop1_2, hop2_0, hop2_1, hop2_2, final, pair_small, ring_small, full_small,
-    send, recv, local, edge_sem, pair_sem, hop_send, hop_recv, fin_sem, sm_sem,
+    arrived, cotv, edge, wp, we, seq, gsw, glu, dgrad, lin, gate, scaled, swished, gainsum, small, total, mean_in, inverse_in,
+    away, pair, part, hop1, hop2, cross, tall, final, pair_small, ring_small, full_small,
+    send, recv, local, edge_sem, pair_sem, hop_sem, cross_sem, tall_sem, fin_sem, sm_sem,
 ):
-    hop1, hop2 = (hop1_0, hop1_1, hop1_2), (hop2_0, hop2_1, hop2_2)
     y, core, x, z = place()
     pos = {"x": x, "y": y, "z": z}
     me = x * 4 + z
@@ -178,23 +184,12 @@
         tile = cotv[pl.ds(r0, 256)]
         tile = jnp.where(frame < live, tile, jnp.zeros_like(tile))
         cotv[pl.ds(r0, 256)] = tile
-        gsw[pl.ds(r0, 256)] = contract_cols(tile, wp[...])
+        gsw[pl.ds(pl.multiple_of(r0 + 16, 16), 256)] = contract_cols(tile, wp[...])
 
     gainsum[...] = jnp.zeros_like(gainsum)
+    total[...] = jnp.zeros_like(total)
     small[...] = jnp.zeros_like(small)
 
-    for k in range(1, 4):
-        for i, (_, _, hops) in enumerate(ROUTES):
-            if k < len(hops):
-                copies[i, k - 1].wait_recv()
-                launch(i, k, relay.at[pl.ds(slot[i, k - 1] * PIECE, PIECE)])
-
-    first.wait()
-    last.wait()
-    rim = jnp.concatenate([edge[0].astype(F32)[:HALO], edge[1].astype(F32)[16 - HALO :]], axis=0)
-    frame = row_frames(FR, 2 * HALO)
-    rim = jnp.where((frame < live) & (frame + me * FR >= 0), rim, 0.0).astype(BF16)
-    gsw[pl.ds(FR, 2 * HALO)] = contract_cols(rim, wp[...])
     column = [counts[j, me] for j in range(16)]
     lane = lax.broadcasted_iota(jnp.int32, (1, CAP), 1)
 
@@ -219,15 +214,37 @@
             got = jnp.dot(pick, rows, preferred_element_type=F32)
             seq[pl.ds(r0, 256)] = got if fresh else seq[pl.ds(r0, 256)] + got
 
-    own.wait()
-    for n, some in enumerate(((3, 4), (2,), (1,))):
-        here = []
+    def forward(k):
+        for i, (_, _, hops) in enumerate(ROUTES):
+            if k < len(hops):
+                copies[i, k - 1].wait_recv()
+                launch(i, k, relay.at[pl.ds(slot[i, k - 1] * PIECE, PIECE)])
+
+    def arrive(steps, more, fresh):
+        here = list(more)
         for i, (offset, _, hops) in enumerate(ROUTES):
-            if len(hops) in some:
-                copies[i, len(hops) - 1].wait_recv()
+            if len(hops) == steps:
+                copies[i, steps - 1].wait_recv()
                 if offset not in here:
                     here.append(offset)
-        collect(here + [(0, 0)] * (n == 0), n == 0)
+        collect(here, fresh)
+
+    forward(1)
+    first.wait()
+    last.wait()
+    rim = jnp.concatenate([edge[0].astype(F32)[:HALO], edge[1].astype(F32)[16 - HALO :]], axis=0)
+    frame = row_frames(FR, 2 * HALO)
+    rim = jnp.where((frame < live) & (frame + me * FR >= 0), rim, 0.0).astype(BF16)
+    rim = contract_cols(rim, wp[...])
+    gsw[FR + 16 : FR + 24] = rim[:HALO]
+    gsw[8:16] = rim[HALO:]
+    own.wait()
+    arrive(1, [(0, 0)], True)
+    forward(2)
+    arrive(2, [], False)
+    forward(3)
+    arrive(3, [], False)
+    arrive(4, [], False)
 
     first = pltpu.make_async_remote_copy(
         seq.at[pl.ds(0, HALO)], seq.at[pl.ds(FR, HALO)], edge_sem.at[4], edge_sem.at[5], device_id=left, device_id_type=MESH)
@@ -245,8 +262,11 @@
             last.wait()
 
         r0 = pl.multiple_of(k * T1, 16)
-        normed, _ = normalize(seq[pl.ds(r0, T1)])
-        scaled[pl.ds(r0, T1)] = (normed * norm_gain[...]).astype(BF16)
+        at = pl.ds(r0, T1)
+        center, inverse = moments(lambda n: seq[at, lanes(n)])
+        mean_in[at], inverse_in[at] = center, inverse
+        for n in range(D // CC):
+            scaled[at, lanes(n)] = ((seq[at, lanes(n)] - center) * inverse * norm_gain[:, lanes(n)]).astype(BF16)
         frame = row_frames(r0, T1)
         valid = (frame < live) & (frame + me * FR >= 0)
 
@@ -276,43 +296,63 @@
             for t in range(KER):
                 term = (wide[4 + t : 4 + t + RC].reshape(RC // 8, 8, CC) * tap[t]).reshape(RC, CC)
                 acc = term if acc is None else acc + term
-            dgrad[pl.ds(pl.multiple_of(r0 + 8, 8), RC), c] = acc
-
-    def middle(depth, gs):
-        normed, inverse = normalize(depth)
-        sc = normed * conv_gain[...]
-        sig = jax.nn.sigmoid(sc)
-        sw = sc * sig
-        gsc = gs * (sig + sw * (1.0 - sig))
-        return norm_back(gsc * conv_gain[...], normed, inverse), sw, gsc * normed
-
-    @pl.loop(0, FR // RT)
+            at = pl.ds(pl.multiple_of(r0 + 8, 8), RC)
+            dgrad[at, c] = acc
+            total[at] += acc
+
+    def middle(at, rows):
+        center = spread(total[at])
+        square = None
+        for n in range(D // CC):
+            off = dgrad[at, lanes(n)] - center
+            square = off * off if square is None else square + off * off
+        inverse = lax.rsqrt(spread(square) + EPS)
+        sum_h = sum_hn = None
+        for n in range(D // CC):
+            gain = conv_gain[:, lanes(n)]
+            normed = (dgrad[at, lanes(n)] - center) * inverse
+            sc = normed * gain
+            sig = jax.nn.sigmoid(sc)
+            sw = sc * sig
+            gsc = gsw[at, lanes(n)] * (sig + sw * (1.0 - sig))
+            h = gsc * gain
+            hn = h * normed
+            gsw[at, lanes(n)] = h
+            dgrad[at, lanes(n)] = normed
+            sum_h = h if sum_h is None else sum_h + h
+            sum_hn = hn if sum_hn is None else sum_hn + hn
+            if rows is not None:
+                swished[rows, lanes(n)] = sw.astype(BF16)
+                gainsum[0, :, lanes(n)] += fold(gsc * normed)
+        sum_h, sum_hn = spread(sum_h), spread(sum_hn)
+        for n in range(D // CC):
+            dgrad[at, lanes(n)] = inverse * (gsw[at, lanes(n)] - sum_h - dgrad[at, lanes(n)] * sum_hn)
+
+    @pl.loop(0, FR // RM)
     def _(k):
-        r0 = pl.multiple_of(k * RT, RT)
-        at = pl.ds(pl.multiple_of(r0 + 16, 16), RT)
-        gd, sw, gc = middle(dgrad[at], gsw[pl.ds(r0, RT)])
-        dgrad[at] = gd
-        swished[pl.ds(r0, RT)] = sw.astype(BF16)
-        gainsum[0] += fold(gc)
-
-    gd, _, _ = middle(
-        jnp.concatenate([dgrad[8:16], dgrad[FR + 16 : FR + 24]], axis=0),
-        jnp.concatenate([gsw[FR + HALO : EXT], gsw[FR : FR + HALO]], axis=0))
-    dgrad[8:16] = gd[:8]
-    dgrad[FR + 16 : FR + 24] = gd[8:]
-
-    def view(p, s, c, cols):
-        index = {"x": slice(None), "z": slice(None), "y": slice(None)}
-        for a in ORDERS[p][:s]:
-            index[a] = pos[a]
-        index[ORDERS[p][s]] = lax.rem(c + 4, 4)
-        return (p, index["x"], index["z"], index["y"], slice(None), cols)
-
-    flying, pairs, done = {}, {}, []
+        r0 = pl.multiple_of(k * RM, RM)
+        middle(pl.ds(pl.multiple_of(r0 + 16, 16), RM), pl.ds(r0, RM))
+
+    middle(slice(8, 16), None)
+    middle(slice(FR + 16, FR + 24), None)
+
+    def block(p, c, cols):
+        c = lax.rem(c + 4, 4)
+        index = (c, slice(None)) if ORDERS[p][0] == "x" else (slice(None), c)
+        return index + (slice(None), slice(None), cols)
+
+    def cell(p, c):
+        c = lax.rem(c + 4, 4)
+        return (x, c) if ORDERS[p][0] == "x" else (c, z)
+
+    def low_high(p):
+        return pl.ds(0, WIDTH[p] // 2), pl.ds(WIDTH[p] // 2, WIDTH[p] // 2)
+
+    flying, crossing, climbing, pairs, finals, done = {}, {}, {}, {}, {}, []
 
     def pair_start(p):
         pairs[p] = pltpu.make_async_remote_copy(
-            away.at[p], pair.at[p], pair_sem.at[0, p], pair_sem.at[1, p], device_id=partner, device_id_type=MESH)
+            away[p], pair[p], pair_sem.at[0, p], pair_sem.at[1, p], device_id=partner, device_id_type=MESH)
         pairs[p].start()
 
     def pair_finish(p):
@@ -321,45 +361,74 @@
         @pl.loop(0, 16)
         def _(i):
             a, b = i // 4, lax.rem(i, 4)
-            part[p, a, b] = (part[p, a, b].astype(F32) + pair[p, a, b].astype(F32)).astype(BF16)
-
-    def step(p, s, n, at, dst, by):
+            part[p][a, b] = (part[p][a, b].astype(F32) + pair[p][a, b].astype(F32)).astype(BF16)
+
+    def step(p, n, at, dst, by):
         c = pltpu.make_async_remote_copy(
-            part.at[at], dst, hop_send.at[p, s, n], hop_recv.at[p, s, n],
-            device_id=along(ORDERS[p][s], by), device_id_type=MESH)
+            part[p].at[at], dst, hop_sem.at[0, p, n], hop_sem.at[1, p, n],
+            device_id=along(ORDERS[p][0], by), device_id_type=MESH)
         c.start()
-        flying[p, s].append(c)
+        flying[p].append(c)
         done.append(c)
 
-    def ring_start(p, s):
-        m = pos[ORDERS[p][s]]
-        flying[p, s] = []
-        step(p, s, 0, view(p, s, m + 2, LO), hop1[s].at[p, 0], 1)
-        step(p, s, 1, view(p, s, m + 2, HI), hop1[s].at[p, 1], -1)
-        step(p, s, 2, view(p, s, m + 1, HI), hop2[s].at[p, 0], 1)
-        step(p, s, 3, view(p, s, m - 1, LO), hop2[s].at[p, 1], -1)
-
-    def ring_middle(p, s):
-        m = pos[ORDERS[p][s]]
-        for n, (by, cols) in enumerate(((1, LO), (-1, HI))):
-            flying[p, s][n].wait_recv()
-            at = view(p, s, m + by, cols)
-            part[at] = (part[at].astype(F32) + hop1[s][p, n].astype(F32)).astype(BF16)
-            step(p, s, 4 + n, at, hop2[s].at[p, 2 + n], by)
-
-    def ring_end(p, s):
-        m = pos[ORDERS[p][s]]
-        for c in flying[p, s][2:]:
+    def ring_start(p):
+        m = pos[ORDERS[p][0]]
+        lo, hi = low_high(p)
+        flying[p] = []
+        step(p, 0, block(p, m + 2, lo), hop1[p].at[0], 1)
+        step(p, 1, block(p, m + 2, hi), hop1[p].at[1], -1)
+        step(p, 2, block(p, m + 1, hi), hop2[p].at[0], 1)
+        step(p, 3, block(p, m - 1, lo), hop2[p].at[1], -1)
+
+    def ring_middle(p):
+        m = pos[ORDERS[p][0]]
+        for n, (by, cols) in enumerate(zip((1, -1), low_high(p))):
+            flying[p][n].wait_recv()
+            at = block(p, m + by, cols)
+            part[p][at] = (part[p][at].astype(F32) + hop1[p][n].astype(F32)).astype(BF16)
+            step(p, 4 + n, at, hop2[p].at[2 + n], by)
+
+    def ring_end(p):
+        m = pos[ORDERS[p][0]]
+        for c in flying[p][2:]:
             c.wait_recv()
-        low, high = view(p, s, m, LO), view(p, s, m, HI)
-        sum_low = part[low].astype(F32) + hop2[s][p, 2].astype(F32) + hop2[s][p, 1].astype(F32)
-        sum_high = part[high].astype(F32) + hop2[s][p, 0].astype(F32) + hop2[s][p, 3].astype(F32)
-        if s < 2:
-            part[low] = sum_low.astype(BF16)
-            part[high] = sum_high.astype(BF16)
-        else:
-            final[core, y, :, p * COLS : p * COLS + HALF] = sum_low.astype(BF16)
-            final[core, y, :, p * COLS + HALF : (p + 1) * COLS] = sum_high.astype(BF16)
+        low, high = (block(p, m, cols) for cols in low_high(p))
+        part[p][low] = (part[p][low].astype(F32) + hop2[p][2].astype(F32) + hop2[p][1].astype(F32)).astype(BF16)
+        part[p][high] = (part[p][high].astype(F32) + hop2[p][0].astype(F32) + hop2[p][3].astype(F32)).astype(BF16)
+        crossing[p] = []
+        for by in (2, 1, 3):
+            c = pltpu.make_async_remote_copy(
+                part[p].at[cell(p, pos[ORDERS[p][1]] + by)], cross[p].at[by - 1], cross_sem.at[0, p, by - 1], cross_sem.at[1, p, by - 1],
+                device_id=along(ORDERS[p][1], by), device_id_type=MESH)
+            c.start()
+            crossing[p].append(c)
+            done.append(c)
+
+    def cross_end(p):
+        for c in crossing[p]:
+            c.wait_recv()
+        total_here = part[p][cell(p, pos[ORDERS[p][1]])].astype(F32)
+        for k in range(3):
+            total_here = total_here + cross[p][k].astype(F32)
+        tall[p][y] = total_here.astype(BF16)
+        climbing[p] = []
+        for by in (2, 1, 3):
+            c = pltpu.make_async_remote_copy(
+                tall[p].at[y], tall[p].at[y], tall_sem.at[0, p, by - 1], tall_sem.at[1, p, by - 1],
+                device_id=along("y", by), device_id_type=MESH)
+            c.start()
+            climbing[p].append(c)
+            done.append(c)
+
+    def tall_end(p):
+        for c in climbing[p]:
+            c.wait_recv()
+        t = [tall[p][k].astype(F32) for k in range(4)]
+        mine = final.at[core, :, :, START[p] : START[p] + WIDTH[p]]
+        mine[...] = (t[0] + t[1]) + (t[2] + t[3])
+        finals[p] = pltpu.make_async_remote_copy(
+            mine, mine, fin_sem.at[0, p], fin_sem.at[1, p], device_id=partner, device_id_type=MESH)
+        finals[p].start()
 
     small_flying = {}
 
@@ -386,23 +455,22 @@
         def _(k):
             value = contract_rows(
                 swished[:, pl.ds(pl.multiple_of(k * 256, 256), 256)], cotv[:, pl.ds(pl.multiple_of(half * 512, 512), 512)])
-            dst[0, k] = value.astype(BF16).reshape(4, 4, 16, COLS)
+            dst[0][k] = value.astype(BF16).reshape(4, 4, 16, WIDTH[0])
 
     project_grad(away, 1 - core)
     pair_start(0)
     project_grad(part, core)
 
-    @pl.loop(0, 4)
-    def _(k):
-        r0 = pl.multiple_of(k * 256, 256)
-        frame = r0 + lax.broadcasted_iota(jnp.int32, (256, 1), 0)
-        projected = jnp.dot(swished[pl.ds(r0, 256)], wp[...], preferred_element_type=F32)
-        swished[pl.ds(r0, 256)] = jnp.where(frame < live, seq[pl.ds(r0, 256)] + projected, 0.0).astype(BF16)
-
-    put_out = pltpu.make_async_copy(swished, layer_out, local.at[4])
-    put_out.start()
+    def project(lo, hi):
+        @pl.loop(lo, hi)
+        def _(k):
+            r0 = pl.multiple_of(k * 256, 256)
+            frame = r0 + lax.broadcasted_iota(jnp.int32, (256, 1), 0)
+            projected = jnp.dot(swished[pl.ds(r0, 256)], wp[...], preferred_element_type=F32)
+            swished[pl.ds(r0, 256)] = jnp.where(frame < live, seq[pl.ds(r0, 256)] + projected, 0.0).astype(BF16)
+
     pair_finish(0)
-    ring_start(0, 0)
+    ring_start(0)
 
     def conv_back(lo, hi):
         @pl.loop(lo, hi)
@@ -432,29 +500,33 @@
             for t in range(KER):
                 small[t : t + 1, c] = jnp.sum(sums[t], axis=0, keepdims=True)
 
-    conv_back(0, 4)
-    ring_middle(0, 0)
-    conv_back(4, 8)
-
-    def expand_grad(dst, half):
+    def expand_grad(dst, p, half):
+        first_col = START[p] - START[1]
+
         @pl.loop(0, 4)
         def _(k):
             value = contract_rows(
                 scaled[pl.ds(0, FR), pl.ds(pl.multiple_of(k * 256, 256), 256)],
-                arrived[pl.ds(pl.multiple_of(half * FR, FR), FR)]).astype(BF16)
-            dst[1, k] = value[:, :COLS].reshape(4, 4, 16, COLS)
-            dst[2, k] = value[:, COLS:].reshape(4, 4, 16, COLS)
-
-    expand_grad(away, 1 - core)
+                arrived[pl.ds(pl.multiple_of(half * FR, FR), FR), first_col : first_col + WIDTH[p]])
+            dst[p][k] = value.astype(BF16).reshape(4, 4, 16, WIDTH[p])
+
+    conv_back(0, 3)
+    ring_middle(0)
+    conv_back(3, 6)
+    expand_grad(away, 1, 1 - core)
     pair_start(1)
+    ring_end(0)
+    expand_grad(part, 1, core)
+    conv_back(6, 8)
+    pair_finish(1)
+    ring_start(1)
+    expand_grad(away, 2, 1 - core)
     pair_start(2)
-    ring_end(0, 0)
-    ring_start(0, 1)
-    expand_grad(part, core)
-    for p in (1, 2):
-        pair_finish(p)
-        ring_start(p, 0)
-    ring_middle(0, 1)
+    cross_end(0)
+    expand_grad(part, 2, core)
+    pair_finish(2)
+    ring_start(2)
+    tall_end(0)
 
     def input_grad(lo, hi):
         @pl.loop(lo, hi)
@@ -462,15 +534,28 @@
             r0 = pl.multiple_of(k * 256, 256)
             grad_scaled = contract_cols(arrived[pl.ds(r0, 256)], we[:, :D]) + contract_cols(
                 arrived[pl.ds(pl.multiple_of(FR + r0, 256), 256)], we[:, D:])
-            normed, inverse = normalize(seq[pl.ds(r0, 256)])
-            gainsum[1] += fold(grad_scaled * normed)
-            cotv[pl.ds(r0, 256)] = (
-                cotv[pl.ds(r0, 256)].astype(F32) + norm_back(grad_scaled * norm_gain[...], normed, inverse)
-            ).astype(BF16)
+            at = pl.ds(r0, 256)
+            gsw[at] = grad_scaled
+            center, inverse = mean_in[at], inverse_in[at]
+            sum_g = sum_gn = None
+            for n in range(D // CC):
+                normed = (seq[at, lanes(n)] - center) * inverse
+                product = gsw[at, lanes(n)] * normed
+                gainsum[1, :, lanes(n)] += fold(product)
+                g = gsw[at, lanes(n)] * norm_gain[:, lanes(n)]
+                gn = product * norm_gain[:, lanes(n)]
+                sum_g = g if sum_g is None else sum_g + g
+                sum_gn = gn if sum_gn is None else sum_gn + gn
+            sum_g, sum_gn = spread(sum_g), spread(sum_gn)
+            for n in range(D // CC):
+                normed = (seq[at, lanes(n)] - center) * inverse
+                g = gsw[at, lanes(n)] * norm_gain[:, lanes(n)]
+                cotv[at, lanes(n)] = (
+                    cotv[at, lanes(n)].astype(F32) + inverse * (g - sum_g - normed * sum_gn)).astype(BF16)
 
     input_grad(0, 2)
-    for p in (1, 2):
-        ring_middle(p, 0)
+    ring_middle(1)
+    ring_middle(2)
     input_grad(2, 4)
     put_grad = pltpu.make_async_copy(cotv, grad_in, local.at[5])
     put_grad.start()
@@ -481,68 +566,62 @@
     small_pair = pltpu.make_async_remote_copy(
         small.at[:, pl.ds(there, 512)], pair_small, sm_sem.at[0, 0], sm_sem.at[1, 0], device_id=partner, device_id_type=MESH)
     small_pair.start()
-    for p in (1, 2):
-        ring_end(p, 0)
-        ring_start(p, 1)
-    ring_end(0, 1)
-    ring_start(0, 2)
+    ring_end(2)
     small_pair.wait()
     small_start(0, small[:, pl.ds(here, 512)] + pair_small[...])
-    for p in (1, 2):
-        ring_middle(p, 1)
-    ring_middle(0, 2)
+    ring_end(1)
+    project(0, 2)
+    cross_end(2)
     small_start(1, small_end(0))
-    for p in (1, 2):
-        ring_end(p, 1)
-        ring_start(p, 2)
-    ring_end(0, 2)
-    for p in (1, 2):
-        ring_middle(p, 2)
+    project(2, 4)
+    put_out = pltpu.make_async_copy(swished, layer_out, local.at[4])
+    put_out.start()
+    cross_end(1)
     small_start(2, small_end(1))
-    for p in (1, 2):
-        ring_end(p, 2)
-
-    gather = []
-    for by in (1, 2, 3):
-        c = pltpu.make_async_remote_copy(
-            final.at[core, y], final.at[core, y], fin_sem.at[0, by - 1], fin_sem.at[1, by - 1],
-            device_id=along("y", by), device_id_type=MESH)
-        c.start()
-        gather.append(c)
+    tall_end(2)
+    tall_end(1)
     full_small[core] = small_end(2)
     small_last = pltpu.make_async_remote_copy(
         full_small.at[core], full_small.at[core], sm_sem.at[0, 10], sm_sem.at[1, 10], device_id=partner, device_id_type=MESH)
     small_last.start()
-    for c in gather:
-        c.wait_recv()
-    final_last = pltpu.make_async_remote_copy(
-        final.at[core], final.at[core], fin_sem.at[0, 3], fin_sem.at[1, 3], device_id=partner, device_id_type=MESH)
-    final_last.start()
-    for c in list(copies.values()) + gather + list(pairs.values()) + done:
+    for c in list(copies.values()) + list(pairs.values()) + done:
         c.wait_send()
     put_out.wait()
     put_grad.wait()
     small_last.wait()
     out_small[:, 0:512] = full_small[0]
     out_small[:, 512:1024] = full_small[1]
-    final_last.wait()
+    for c in finals.values():
+        c.wait()
     out_sum[...] = final[...]
 
 
-def finish_kernel(layer_in, grad_src, sums, small, layer_out, grad_in, expand, project, taps, norm_gain, conv_gain):
-    layer_out[0] = layer_in[...]
-    grad_in[0] = grad_src[...]
-
-    @pl.when(pl.program_id(0) == 0)
-    def _():
+def finish_kernel(
+    layer_in, grad_src, sums, small, layer_out, grad_in, expand, project, taps, norm_gain, conv_gain, rows, get_sem, put_sem,
+):
+    gets, puts = [], []
+    for i, src in enumerate((layer_in, grad_src)):
         for k in range(4):
-            for c in range(2):
-                rows = sums[c, k].astype(F32)
-                project[k * 16 : k * 16 + 16, c * 512 : (c + 1) * 512] = rows[:, :512]
-                expand[k * 16 : k * 16 + 16, c * 1024 : (c + 1) * 1024] = rows[:, 512:]
-        taps[...] = small[0:KER]
-        norm_gain[...] = small[9:10]
-        conv_gain[...] = small[10:11]
+            at = pl.ds(k * 256, 256)
+            c = pltpu.make_async_copy(src.at[at], rows.at[i, at], get_sem.at[i, k])
+            c.start()
+            gets.append((i, k, c))
+    for k in range(4):
+        for c in range(2):
+            values = sums[c, k]
+            project[k * 16 : k * 16 + 16, c * 512 : (c + 1) * 512] = values[:, :512]
+            expand[k * 16 : k * 16 + 16, c * 1024 : (c + 1) * 1024] = values[:, 512:]
+    taps[...] = small[0:KER]
+    norm_gain[...] = small[9:10]
+    conv_gain[...] = small[10:11]
+    for i, k, c in gets:
+        c.wait()
+        at = pl.ds(k * 256, 256)
+        put = pltpu.make_async_copy(rows.at[i, at], (layer_out, grad_in)[i].at[0, at], put_sem.at[i, k])
+        put.start()
+        puts.append(put)
+    for put in puts:
+        put.wait()
 
 
 def per_device(
@@ -552,8 +631,8 @@
     vmem = pl.BlockSpec(memory_space=pltpu.VMEM)
     smem = pl.BlockSpec(memory_space=pltpu.SMEM)
 
-    def hop_shapes(n):
-        return [pltpu.VMEM((3, n) + (4,) * (2 - s) + (16, HALF), BF16) for s in range(3)]
+    def each(shape_of):
+        return tuple(pltpu.VMEM(shape_of(w), BF16) for w in WIDTH)
 
     layer_out, grad_in, _, sums, small = pl.pallas_call(
         kernel,
@@ -561,7 +640,7 @@
             jax.ShapeDtypeStruct((FR, D), BF16),
             jax.ShapeDtypeStruct((FR, D), BF16),
             jax.ShapeDtypeStruct((N_RELAY * PIECE, D), BF16),
-            jax.ShapeDtypeStruct((2, 4, 16, 3 * COLS), BF16),
+            jax.ShapeDtypeStruct((2, 4, 16, sum(WIDTH)), F32),
             jax.ShapeDtypeStruct((16, D), F32),
         ],
         in_specs=[any_space, any_space, smem, smem, vmem, any_space, vmem, vmem, any_space],
@@ -573,7 +652,7 @@
             pltpu.VMEM((D, D), BF16),
             pltpu.VMEM((D, 2 * D), BF16),
             pltpu.VMEM((EXT, D), F32),
-            pltpu.VMEM((EXT, D), F32),
+            pltpu.VMEM((FR + 32, D), F32),
             pltpu.VMEM((FR + 32, D), F32),
             pltpu.VMEM((FR + 32, D), F32),
             pltpu.VMEM((EXT, D), F32),
@@ -582,12 +661,15 @@
             pltpu.VMEM((FR, D), BF16),
             pltpu.VMEM((2, 8, D), F32),
             pltpu.VMEM((16, D), F32),
-            pltpu.VMEM((3, 4, 4, 4, 16, COLS), BF16),
-            pltpu.VMEM((3, 4, 4, 4, 16, COLS), BF16),
-            pltpu.VMEM((3, 4, 4, 4, 16, COLS), BF16),
-            *hop_shapes(2),
-            *hop_shapes(4),
-            pltpu.VMEM((2, 4, 16, 3 * COLS), BF16),
+            pltpu.VMEM((FR + 32, CC), F32),
+            pltpu.VMEM((EXT, CC), F32),
+            pltpu.VMEM((EXT, CC), F32),
+            *[each(lambda w: (4, 4, 4, 16, w)) for _ in range(3)],
+            each(lambda w: (2, 4, 4, 16, w // 2)),
+            each(lambda w: (4, 4, 4, 16, w // 2)),
+            each(lambda w: (3, 4, 16, w)),
+            each(lambda w: (4, 4, 16, w)),
+            pltpu.VMEM((2, 4, 16, sum(WIDTH)), F32),
             pltpu.VMEM((16, 512), F32),
             pltpu.VMEM((3, 4, 16, 512), F32),
             pltpu.VMEM((2, 16, 512), F32),
@@ -596,9 +678,10 @@
             DMA((6,)),
             DMA((8,)),
             DMA((2, 3)),
-            DMA((3, 3, 6)),
-            DMA((3, 3, 6)),
-            DMA((2, 4)),
+            DMA((2, 3, 6)),
+            DMA((2, 3, 3)),
+            DMA((2, 3, 3)),
+            DMA((2, 3)),
             DMA((2, 11)),
         ],
         compiler_params=pltpu.CompilerParams(collective_id=0, has_side_effects=True, vmem_limit_bytes=VMEM_LIMIT),
@@ -617,9 +700,10 @@
             jax.ShapeDtypeStruct((1, D), F32),
             jax.ShapeDtypeStruct((1, D), F32),
         ],
-        grid=(4,),
-        in_specs=[pl.BlockSpec((FR // 4, D), lambda i: (i, 0))] * 2 + [vmem] * 2,
-        out_specs=[pl.BlockSpec((1, FR // 4, D), lambda i: (0, i, 0))] * 2 + [vmem] * 5,
+        in_specs=[any_space] * 2 + [vmem] * 2,
+        out_specs=[any_space] * 2 + [vmem] * 5,
+        scratch_shapes=[pltpu.VMEM((2, FR, D), BF16), DMA((2, 4)), DMA((2, 4))],
+        compiler_params=pltpu.CompilerParams(vmem_limit_bytes=VMEM_LIMIT),
     )(layer_out, grad_in, sums, small)
     return layer_out, grad_in, expand, project, taps, norm_gain[0], conv_gain[0]
 

time: 150 us -> 143 us (0.953)
  Pallas kernels: 149 us -> 142 us
    pallas_call x1, Pallas kernels: 144 us -> 136 us  [per_device(): pl.pallas_call(kernel, out_shape=[jax.ShapeDtypeStruct((FR, D), BF16), ja...]
where the time goes in v3:
time: 143 us
  Pallas kernels  142 us (99%)
    pallas_call x1, Pallas kernels, per_device(): pl.pallas_call(kernel, out_shape=[jax.ShapeDtypeStruct((FR, D), BF16), ja...  136 us
    pallas_call x1, Pallas kernels, per_device(): pl.pallas_call(finish_kernel, out_shape=[jax.ShapeDtypeStruct((1, FR, D),...  5.61 us

profile of v3, /device:TPU:1, one launch (start us, length us, event | category | flops | bytes accessed | tf_op | source)
XLA Modules:
  0.0 142.8 jit_solution(1778419174705734966)
XLA Ops:
  1.3 135.9 %shard_map.144 = (bf16[1024,1024]{1,0:T(8,128)(2,1)}, bf16[1024,1024]{1,0:T(8,128)(2,1)}, bf16[2176,1024]{1,0:T(8,128)(2,1)}, f32[2,4,16,1536]{3,2,1,0:T(8,128)}, f32[16,1024]{1,0:T(8,128)}) custom-call(bf16[2048,1024]{1,0:T(8,128)(2,1)} %bitcast.7, bf16[1024,1024]{1,0:T(8,128)(2,1)} %bitcast.8, s32[16,16]{1,0:T(8,128)} %bitcast.9, s32[1]{0:T(128)S(6)} %copy.16.length, ...), custom_call_target="tpu_custom_call" | custom-call | tf_op jit(solution)/shard_map/pallas_call | solution.py:637
  137.2 5.6 %shard_map.145 = (bf16[1,1024,1024]{2,1,0:T(8,128)(2,1)}, bf16[1,1024,1024]{2,1,0:T(8,128)(2,1)}, f32[64,2048]{1,0:T(8,128)}, f32[64,1024]{1,0:T(8,128)}, f32[9,...) custom-call(bf16[1024,1024]{1,0:T(8,128)(2,1)} %get-tuple-element.18.layer_in, ...), custom_call_target="tpu_custom_call" | custom-call | tf_op jit(solution)/shard_map/pallas_call | solution.py:692

commit v4 on v3

--- a/solution.py
+++ b/solution.py
@@ -114,9 +114,9 @@
 
 
 def kernel(
-    loader, cot, counts, length, norm_gain, w_expand, taps, conv_gain, w_project,
+    loader, cot, counts, length, norm_gain_in, w_expand, taps_in, conv_gain_in, w_project,
     layer_out, grad_in, relay, out_sum, out_small,
-    arrived, cotv, edge, wp, we, seq, gsw, glu, dgrad, lin, gate, scaled, swished, gainsum, small, total, mean_in, inverse_in,
+    arrived, cotv, edge, wp, we, seq, gsw, glu, dgrad, lin, gate, scaled, swished, gainsum, small, total, mean_in, inverse_in, norm_gain, taps, conv_gain,
     away, pair, part, hop1, hop2, cross, tall, final, pair_small, ring_small, full_small,
     send, recv, local, edge_sem, pair_sem, hop_sem, cross_sem, tall_sem, fin_sem, sm_sem,
 ):
@@ -172,7 +172,11 @@
     get_cot = pltpu.make_async_copy(cot, cotv, local.at[1])
     get_wp = pltpu.make_async_copy(w_project, wp, local.at[2])
     get_we = pltpu.make_async_copy(w_expand, we, local.at[3])
-    for c in (get_cot, get_wp, own, get_we):
+    get_small = [
+        pltpu.make_async_copy(src, dst, local.at[6 + i])
+        for i, (src, dst) in enumerate(((norm_gain_in, norm_gain), (taps_in, taps), (conv_gain_in, conv_gain)))
+    ]
+    for c in [get_cot, get_wp, own, get_we] + get_small:
         c.start()
     get_cot.wait()
     get_wp.wait()
@@ -252,7 +256,8 @@
         seq.at[pl.ds(FR - HALO, HALO)], seq.at[pl.ds(FR + HALO, HALO)], edge_sem.at[6], edge_sem.at[7], device_id=right, device_id_type=MESH)
     first.start()
     last.start()
-    get_we.wait()
+    for c in [get_we] + get_small:
+        c.wait()
 
     @pl.loop(0, EXT // T1)
     def _(k):
@@ -596,32 +601,20 @@
     out_sum[...] = final[...]
 
 
-def finish_kernel(
-    layer_in, grad_src, sums, small, layer_out, grad_in, expand, project, taps, norm_gain, conv_gain, rows, get_sem, put_sem,
-):
-    gets, puts = [], []
-    for i, src in enumerate((layer_in, grad_src)):
+def finish_kernel(layer_in, grad_src, sums, small, layer_out, grad_in, expand, project, taps, norm_gain, conv_gain):
+    layer_out[0] = layer_in[...]
+    grad_in[0] = grad_src[...]
+
+    @pl.when(pl.program_id(0) == 0)
+    def _():
         for k in range(4):
-            at = pl.ds(k * 256, 256)
-            c = pltpu.make_async_copy(src.at[at], rows.at[i, at], get_sem.at[i, k])
-            c.start()
-            gets.append((i, k, c))
-    for k in range(4):
-        for c in range(2):
-            values = sums[c, k]
-            project[k * 16 : k * 16 + 16, c * 512 : (c + 1) * 512] = values[:, :512]
-            expand[k * 16 : k * 16 + 16, c * 1024 : (c + 1) * 1024] = values[:, 512:]
-    taps[...] = small[0:KER]
-    norm_gain[...] = small[9:10]
-    conv_gain[...] = small[10:11]
-    for i, k, c in gets:
-        c.wait()
-        at = pl.ds(k * 256, 256)
-        put = pltpu.make_async_copy(rows.at[i, at], (layer_out, grad_in)[i].at[0, at], put_sem.at[i, k])
-        put.start()
-        puts.append(put)
-    for put in puts:
-        put.wait()
+            for c in range(2):
+                rows = sums[c, k]
+                project[k * 16 : k * 16 + 16, c * 512 : (c + 1) * 512] = rows[:, :512]
+                expand[k * 16 : k * 16 + 16, c * 1024 : (c + 1) * 1024] = rows[:, 512:]
+        taps[...] = small[0:KER]
+        norm_gain[...] = small[9:10]
+        conv_gain[...] = small[10:11]
 
 
 def per_device(
@@ -643,7 +636,7 @@
             jax.ShapeDtypeStruct((2, 4, 16, sum(WIDTH)), F32),
             jax.ShapeDtypeStruct((16, D), F32),
         ],
-        in_specs=[any_space, any_space, smem, smem, vmem, any_space, vmem, vmem, any_space],
+        in_specs=[any_space, any_space, smem, smem] + [any_space] * 5,
         out_specs=[any_space] * 3 + [vmem] * 2,
         scratch_shapes=[
             pltpu.VMEM((16 * CAP, D), BF16),
@@ -664,6 +657,9 @@
             pltpu.VMEM((FR + 32, CC), F32),
             pltpu.VMEM((EXT, CC), F32),
             pltpu.VMEM((EXT, CC), F32),
+            pltpu.VMEM((1, D), F32),
+            pltpu.VMEM((KER, D), F32),
+            pltpu.VMEM((1, D), F32),
             *[each(lambda w: (4, 4, 4, 16, w)) for _ in range(3)],
             each(lambda w: (2, 4, 4, 16, w // 2)),
             each(lambda w: (4, 4, 4, 16, w // 2)),
@@ -675,7 +671,7 @@
             pltpu.VMEM((2, 16, 512), F32),
             DMA((N_HOPS,)),
             DMA((N_HOPS,)),
-            DMA((6,)),
+            DMA((9,)),
             DMA((8,)),
             DMA((2, 3)),
             DMA((2, 3, 6)),
@@ -700,10 +696,9 @@
             jax.ShapeDtypeStruct((1, D), F32),
             jax.ShapeDtypeStruct((1, D), F32),
         ],
-        in_specs=[any_space] * 2 + [vmem] * 2,
-        out_specs=[any_space] * 2 + [vmem] * 5,
-        scratch_shapes=[pltpu.VMEM((2, FR, D), BF16), DMA((2, 4)), DMA((2, 4))],
-        compiler_params=pltpu.CompilerParams(vmem_limit_bytes=VMEM_LIMIT),
+        grid=(2,),
+        in_specs=[pl.BlockSpec((FR // 2, D), lambda i: (i, 0))] * 2 + [vmem] * 2,
+        out_specs=[pl.BlockSpec((1, FR // 2, D), lambda i: (0, i, 0))] * 2 + [vmem] * 5,
     )(layer_out, grad_in, sums, small)
     return layer_out, grad_in, expand, project, taps, norm_gain[0], conv_gain[0]
 

time: 143 us -> 142 us (level)
  Pallas kernels: 142 us -> 140 us
where the time goes in v4:
time: 142 us; the launch traced here: 141 us
  Pallas kernels  140 us (99%)
    pallas_call x1, Pallas kernels, per_device(): pl.pallas_call(kernel, out_shape=[jax.ShapeDtypeStruct((FR, D), BF16), ja...  136 us
    pallas_call x1, Pallas kernels, per_device(): pl.pallas_call(finish_kernel, out_shape=[jax.ShapeDtypeStruct((1, FR, D),...  4.26 us

profile of v4, /device:TPU:1, one launch (start us, length us, event | category | flops | bytes accessed | tf_op | source)
XLA Modules:
  0.0 141.5 jit_solution(4601933657520420792)
XLA Ops:
  1.3 135.9 %shard_map.144 = (bf16[1024,1024]{1,0:T(8,128)(2,1)}, bf16[1024,1024]{1,0:T(8,128)(2,1)}, bf16[2176,1024]{1,0:T(8,128)(2,1)}, f32[2,4,16,1536]{3,2,1,0:T(8,128)}, f32[16,1024]{1,0:T(8,128)}) custom-call(bf16[2048,1024]{1,0:T(8,128)(2,1)} %bitcast.7, bf16[1024,1024]{1,0:T(8,128)(2,1)} %bitcast.8, s32[16,16]{1,0:T(8,128)} %bitcast.9, s32[1]{0:T(128)S(6)} %copy.16.length, ...), custom_call_target="tpu_custom_call" | custom-call | tf_op jit(solution)/shard_map/pallas_call | solution.py:630
  137.2 4.3 %shard_map.145 = (bf16[1,1024,1024]{2,1,0:T(8,128)(2,1)}, bf16[1,1024,1024]{2,1,0:T(8,128)(2,1)}, f32[64,2048]{1,0:T(8,128)}, f32[64,1024]{1,0:T(8,128)}, f32[9,...) custom-call(bf16[1024,1024]{1,0:T(8,128)(2,1)} %get-tuple-element.18.layer_in, ...), custom_call_target="tpu_custom_call" | custom-call | tf_op jit(solution)/shard_map/pallas_call | solution.py:688
